TPU v7x, 512 devices: a whole 4x4x16 slice. The times are simulated.
512 devices in a mesh: grp: 16 (over y_hi, x, core), blk: 32 (over y_lo, z).
Axes of the slice: x: 4, y: 4 (y_hi: 2, y_lo: 2; y = y_hi * 2 + y_lo), z: 16, core: 2. Of those that a mesh axis runs over, the one named last changes fastest.
Arguments:
- video_encoder_output: bfloat16 [65536, 1024], P(('grp', 'blk')), may hold values from -3 to 3
- caption_encoder_output: bfloat16 [65536, 1024], P(('grp', 'blk')), may hold values from -3 to 3
- video_map_matrix: bfloat16 [1024, 1024], replicated, may hold values from -0.1875 to 0.1875
- caption_map_matrix: bfloat16 [1024, 1024], replicated, may hold values from -0.1875 to 0.1875
- matching_caption: int32 [65536], P('grp'), may hold values from 0 to 4095
- score_multiplier: float32 [1], replicated, may hold values from 32 to 64
- score_offset: float32 [1], replicated, may hold values from -5 to -3
Outputs:
- clip_hidden_grad: bfloat16 [65536, 1024], P(('grp', 'blk'))
- text_hidden_grad: bfloat16 [65536, 1024], P(('grp', 'blk'))
- clip_weight_grad: float32 [1024, 1024], P('blk')
- text_weight_grad: float32 [1024, 1024], P('blk')
Inputs may be any that keep to these rules, and one draw needn't show every extreme that they name: `matching_caption`: each entry indexes the positive commentary of that clip within the clip's own group of 4096 pairs, counted from 0 in that group; several clips may share one commentary, and some commentaries are the positive of no clip.
All inputs are finite; a program needn't handle non-finite values.
Results may differ from a plain program's by a relative error of at most 0.015.
Values may be sent and summed in bfloat16 or wider, within the bound.
A program may use at most 64 MiB of HBM per device.

v0:
```python
import jax
import jax.numpy as jnp
from jax import lax
from jax.sharding import PartitionSpec as P


def project(hidden, weight):
    raw_value = jnp.dot(hidden, weight, preferred_element_type=jnp.float32)
    length = jnp.sqrt(jnp.sum(raw_value * raw_value, axis=1, keepdims=True) + 1e-06)
    return (length, raw_value / length)


def factor_matrix(
    left_operand, right_operand, left_location, right_begin, score_scaled, shift_amount
):
    pair_scores = (
        score_scaled
        * lax.dot_general(
            left_operand,
            right_operand,
            (((1,), (1,)), ((), ())),
            preferred_element_type=jnp.float32,
        )
        + shift_amount
    )
    columns = right_begin + jnp.arange(right_operand.shape[0], dtype=jnp.int32)
    match_polarity = jnp.where(left_location[:, None] == columns[None, :], 1.0, -1.0).astype(
        jnp.float32
    )
    return (-match_polarity * jax.nn.sigmoid(-match_polarity * pair_scores) * score_scaled).astype(
        jnp.bfloat16
    )


def transposed_product(coef_block, emb_block):
    return lax.dot_general(
        coef_block, emb_block, (((0,), (0,)), ((), ())), preferred_element_type=jnp.float32
    )


def tower_back(hidden, weight, emb_grad, length, unit_vec):
    radial = jnp.sum(unit_vec * emb_grad, axis=1, keepdims=True)
    raw_grad = ((emb_grad - unit_vec * radial) / length).astype(jnp.bfloat16)
    hidden_grad = lax.dot_general(
        raw_grad, weight, (((1,), (1,)), ((), ())), preferred_element_type=jnp.float32
    ).astype(jnp.bfloat16)
    device_term = transposed_product(hidden, raw_grad)
    rounded = lax.optimization_barrier(device_term.astype(jnp.bfloat16))
    return (hidden_grad, rounded.astype(jnp.float32))


def local(
    video_encoder_output,
    caption_encoder_output,
    video_map_matrix,
    caption_map_matrix,
    matching_caption,
    score_multiplier,
    score_offset,
):
    score_scaled = score_multiplier[0]
    shift_amount = score_offset[0]
    own_count = video_encoder_output.shape[0]
    local_begin = lax.axis_index("blk") * own_count
    clip_length, clip_unit = project(video_encoder_output, video_map_matrix)
    text_length, text_unit = project(caption_encoder_output, caption_map_matrix)
    video_vector = clip_unit.astype(jnp.bfloat16)
    caption_vector = text_unit.astype(jnp.bfloat16)
    local_location = lax.dynamic_slice_in_dim(matching_caption, local_begin, own_count)
    video_slice = lax.all_gather(video_vector, "blk", axis=0, tiled=True)
    caption_slice = lax.all_gather(caption_vector, "blk", axis=0, tiled=True)
    source_factor = factor_matrix(
        video_vector, caption_slice, local_location, jnp.int32(0), score_scaled, shift_amount
    )
    clip_acc = jnp.dot(source_factor, caption_slice, preferred_element_type=jnp.float32)
    target_factor = factor_matrix(
        video_slice, caption_vector, matching_caption, local_begin, score_scaled, shift_amount
    )
    text_acc = transposed_product(target_factor, video_slice)
    clip_hgrad, clip_term = tower_back(
        video_encoder_output, video_map_matrix, clip_acc, clip_length, clip_unit
    )
    text_hgrad, text_term = tower_back(
        caption_encoder_output, caption_map_matrix, text_acc, text_length, text_unit
    )
    shards = (
        lax.psum_scatter(
            clip_term.astype(jnp.bfloat16), "blk", scatter_dimension=0, tiled=True
        ).astype(jnp.float32),
        lax.psum_scatter(
            text_term.astype(jnp.bfloat16), "blk", scatter_dimension=0, tiled=True
        ).astype(jnp.float32),
    )
    clip_wgrad, text_weight_gradient = (
        lax.psum(shards[0].astype(jnp.bfloat16), "grp").astype(jnp.float32),
        lax.psum(shards[1].astype(jnp.bfloat16), "grp").astype(jnp.float32),
    )
    return (clip_hgrad, text_hgrad, clip_wgrad, text_weight_gradient)


def solution(mesh):
    placed = (P(("grp", "blk"), None), P(("grp", "blk"), None), P(), P(), P("grp"), P(), P())
    return jax.shard_map(
        local,
        mesh=mesh,
        in_specs=placed,
        out_specs=(
            P(("grp", "blk"), None),
            P(("grp", "blk"), None),
            P("blk", None),
            P("blk", None),
        ),
        check_vma=False,
    )
```

profile of v0, /device:TPU:1, one launch (start us, length us, event | category | flops | bytes accessed | tf_op | source)
XLA Modules:
  0.0 736.0 jit_solution(7955400065342535856)
XLA Ops:
  7.2 1.5 copy-done
  8.8 1.5 multiply_reduce_fusion.3
  10.2 0.8 fusion.35
  11.2 2.1 multiply_reduce_fusion.2
  13.3 0.8 fusion.36
  14.1 0.0 reduce-scatter.9.cloned.1.call-start
  15.5 130.1 %all-gather.5.cloned.1.call-done = bf16[4096,1024]{1,0:T(8,128)(2,1)} async-done(((bf16[128,1024]{1,0:T(8,128)(2,1)}), bf16[4096,1024]{1,0:T(8,128)(2,1)}) %all-gather.5.cloned.1.call-update) | async-done | bytes 8388624 | tf_op jit(solution)/shard_map/all_gather | solution.py:70
  145.6 12.1 %multiply_reduce_fusion = (f32[128]{0:T(128)S(1)}, f32[128,1024]{1,0:T(8,128)}) fusion(f32[128,1024]{1,0:T(8,128)S(1)} %get-tuple-element.15, f32[128]{0:T(128)S(1)} %add_sqrt_fusion, bf16[4096,1024]{1,0:T(8,128)(2,1)} %all-gather.5.cloned.1.call-done, bf16[128,1024]{1,0:T(8,128)(2,1)} %fusion.36, f32[]{:T(128)} %bitcast.25, f32[]{:T(128)} %bitcast.23, ...), kind=kOutput, calls=%fused_computation.39 | convolution fusion | flops 2154168320 | bytes 9717256 | tf_op jit(solution)/shard_map/dot_general | solution.py:36
  157.7 3.2 convert_bitcast_fusion
  160.8 3.9 copy.17
  164.8 0.1 dynamic_slice.3
  164.9 125.9 %all-gather.3.cloned.1.call-done = bf16[4096,1024]{1,0:T(8,128)(2,1)} async-done(((bf16[128,1024]{1,0:T(8,128)(2,1)}), bf16[4096,1024]{1,0:T(8,128)(2,1)}) %all-gather.3.cloned.1.call-update) | async-done | bytes 8388624 | tf_op jit(solution)/shard_map/all_gather | solution.py:71
  290.8 10.9 %multiply_reduce_fusion.1 = (f32[128]{0:T(128)S(1)}, f32[128,1024]{1,0:T(8,128)}) fusion(f32[128,1024]{1,0:T(8,128)S(1)} %get-tuple-element.17, f32[128]{0:T(128)S(1)} %add_sqrt_fusion.1, bf16[4096,1024]{1,0:T(8,128)(2,1)} %all-gather.3.cloned.1.call-done, bf16[128,1024]{1,0:T(8,128)(2,1)S(1)} %copy-done.1, f32[]{:T(128)} %bitcast.24, f32[]{:T(128)} %bitcast.22, ...), kind=kOutput, calls=%fused_computation.41 | convolution fusion | flops 2154168320 | bytes 9700872 | tf_op jit(solution)/shard_map/dot_general | solution.py:75
  301.8 3.2 convert_bitcast_fusion.1
  305.0 3.9 copy.15
  309.0 2.6 convolution_convert_fusion.1
  311.6 111.7 %reduce-scatter.9.cloned.1.call-done = bf16[32,1024]{1,0:T(8,128)(2,1)} async-done(((bf16[1024,1024]{1,0:T(8,128)(2,1)}), bf16[32,1024]{1,0:T(8,128)(2,1)}) %reduce-scatter.9.cloned.1.call-update) | async-done | bytes 65552
  423.3 1.7 copy.18
  424.9 130.3 %reduce-scatter.7.cloned.1.call-done = bf16[32,1024]{1,0:T(8,128)(2,1)} async-done(((bf16[1024,1024]{1,0:T(8,128)(2,1)}), bf16[32,1024]{1,0:T(8,128)(2,1)}) %reduce-scatter.7.cloned.1.call-update) | async-done | bytes 65552
  555.2 1.7 copy.16
  556.9 3.3 convolution_convert_fusion
  560.2 165.8 %all-reduce.3.cloned.1.call-done = (bf16[32,1024]{0,1:T(8,128)(2,1)}, bf16[32,1024]{0,1:T(8,128)(2,1)}) async-done(((bf16[32,1024]{0,1:T(8,128)(2,1)}, bf16[32,1024]{0,1:T(8,128)(2,1)}), (bf16[32,1024]{0,1:T(8,128)(2,1)}, bf16[32,1024]{0,1:T(8,128)(2,1)})) %all-reduce.3.cloned.1.call-update) | async-done | bytes 131088 | tf_op jit(solution)/shard_map/psum | solution.py:95
  726.0 1.7 copy.13
  727.7 1.7 copy.14
  (19 shorter events, 0.3 us)
Async XLA Ops:
  7.2 1.6 copy-start
  7.2 4.0 copy-start.2
  7.2 138.4 %all-gather.5.cloned.1.call-start = ((), (), s32[]{:S(2)}) async-start(), calls=%async_computation.3 | async-start | bytes 8650752 | tf_op jit(solution)/shard_map/all_gather | solution.py:70
  11.1 134.5 %copy-start.3 = (s32[4096]{0:T(1024)S(1)}, s32[4096]{0:T(1024)}, u32[]{:S(2)}) copy-start(s32[4096]{0:T(1024)} %param.11) | copy-start | bytes 49156
  11.1 279.7 %all-gather.3.cloned.1.call-start = ((), (), s32[]{:S(2)}) async-start(), calls=%async_computation.2 | async-start | bytes 8650752 | tf_op jit(solution)/shard_map/all_gather | solution.py:71
  14.1 409.1 %reduce-scatter.9.cloned.1.call-start = ((), (), s32[]{:S(2)}) async-start(), calls=%async_computation.5 | async-start | bytes 2162688
  164.8 126.1 %copy-start.1 = (bf16[128,1024]{1,0:T(8,128)(2,1)S(1)}, bf16[128,1024]{1,0:T(8,128)(2,1)}, u32[]{:S(2)}) copy-start(bf16[128,1024]{1,0:T(8,128)(2,1)} %fusion.35) | copy-start | bytes 786436
  164.8 390.4 %reduce-scatter.7.cloned.1.call-start = ((), (), s32[]{:S(2)}) async-start(), calls=%async_computation.4 | async-start | bytes 2162688
  309.0 417.0 %all-reduce.3.cloned.1.call-start = ((), (), s32[]{:S(2)}) async-start(), calls=%async_computation.6 | async-start | bytes 1048576 | tf_op jit(solution)/shard_map/psum | solution.py:95
Sparse Core Ops, SparseCore 0:
  11.2 134.3 all-gather.4
  148.3 142.5 all-gather.2
  293.6 129.5 reduce-scatter.8
  426.1 129.0 reduce-scatter.6
  558.0 167.9 all-reduce.2
where the time goes:
time: 737 us; the launch traced here: 736 us
  waiting for transfers between devices  664 us (90%)
  matrix products  38.9 us (5%)
  local copies, waits for them, and re-layouts  16.3 us (2%)
  between operations  15.1 us (2%)
    unnamed x7, waiting for transfers between devices  242 us
    psum x1, waiting for transfers between devices, local(): lax.psum(shards[0].astype(jnp.bfloat16), 'grp').astype(jnp.float32)  166 us
    all_gather x1, waiting for transfers between devices, local(): video_slice = lax.all_gather(video_vector, 'blk', axis=0, tiled=True)  130 us
    all_gather x1, waiting for transfers between devices, local(): caption_slice = lax.all_gather(caption_vector, 'blk', axis=0, tiled=True)  126 us
    dot_general x3, matrix products, transposed_product(): lax.dot_general(coef_block, emb_block, (((0,), (0,)), ((), ())), preferre...  18.5 us
    unnamed x14, local copies, waits for them, and re-layouts  16.2 us
  transfers between devices with their start and end apart: 5, of which 5 were waited for; matrix products, arithmetic and copies ran while one was open for 7% of the time, Pallas kernels for 0%

commit v1 on v0

v1 whole, which is shorter than its diff:
```python
import jax
import jax.numpy as jnp
from jax import lax
from jax.experimental import pallas as pl
from jax.experimental.pallas import tpu as pltpu
from jax.sharding import PartitionSpec as P

MESH = pl.DeviceIdType.MESH
F32 = jnp.float32
BF16 = jnp.bfloat16
NX, NZ, TOK, D, E = 4, 16, 128, 1024, 1024
HALF = TOK // 2
CLIP, TEXT = 0, 1


def kernel(
    hv_hbm,
    hc_hbm,
    wv_hbm,
    wc_hbm,
    match_ref,
    scale_ref,
    shift_ref,
    clip_hid,
    text_hid,
    clip_wg,
    text_wg,
    w,
    hx,
    ht,
    unit,
    length,
    tt,
    emb,
    part,
    cacc,
    back_in,
    back_out,
    share_out,
    share_in,
    g_out,
    g_in,
    y_out,
    y_in,
    z_out,
    z_in,
    f_all,
    load_sem,
    ring_s,
    ring_r,
    back_s,
    back_r,
    share_s,
    share_r,
    hid_s,
    hid_r,
    rel_s,
    rel_r,
    ga_s,
    ga_r,
    yb_s,
    yb_r,
    zc_s,
    zc_r,
    fd_s,
    fd_r,
):
    grp = lax.axis_index("grp")
    blk = lax.axis_index("blk")
    yh, x, core = grp // 8, (grp // 2) % 4, grp % 2
    yl, z = blk // NZ, blk % NZ
    y = yh * 2 + yl
    q = x * 2 + core

    def place(x=x, y=y, z=z, core=core):
        return ((y // 2) * 8 + x * 2 + core, (y % 2) * NZ + z)

    right, left = place(z=(z + 1) % NZ), place(z=(z + NZ - 1) % NZ)
    partner = place(y=yh * 2 + 1 - yl)
    sibling = place(core=1 - core)

    def remote(src, dst, s, r, device):
        return pltpu.make_async_remote_copy(
            src_ref=src, dst_ref=dst, send_sem=s, recv_sem=r, device_id=device, device_id_type=MESH
        )

    loads = [
        pltpu.make_async_copy(wc_hbm, w.at[TEXT], load_sem.at[0]),
        pltpu.make_async_copy(hc_hbm, hx.at[TEXT, q], load_sem.at[1]),
        pltpu.make_async_copy(wv_hbm, w.at[CLIP], load_sem.at[2]),
        pltpu.make_async_copy(hv_hbm, hx.at[CLIP, q], load_sem.at[3]),
    ]
    for copy in loads:
        copy.start()

    barrier = pltpu.get_barrier_semaphore()

    @pl.loop(1, NZ)
    def _(o):
        pl.semaphore_signal(barrier, 1, device_id=place(z=(z + o) % NZ), device_id_type=MESH)
        pl.semaphore_signal(barrier, 1, device_id=((grp + o) % 16, blk), device_id_type=MESH)

    pl.semaphore_signal(barrier, 1, device_id=place(y=(y + 1) % 4), device_id_type=MESH)
    pl.semaphore_signal(barrier, 1, device_id=place(y=(y + 3) % 4), device_id_type=MESH)

    def project(tower):
        raw = jnp.dot(hx[tower, q], w[tower], preferred_element_type=F32)
        size = jnp.sqrt(jnp.sum(raw * raw, axis=1, keepdims=True) + 1e-06)
        vec = raw / size
        unit[tower] = vec
        length[tower] = size
        return vec.astype(BF16)

    def ring(d, k, c):
        src = tt.at[k - 1, pl.ds((0 if isinstance(k, int) and k == 1 else TOK * d) + HALF * c, HALF)]
        dst = tt.at[k, pl.ds((0 if isinstance(k, int) and k == 8 else TOK * d) + HALF * c, HALF)]
        return remote(src, dst, ring_s.at[d, k - 1, c], ring_r.at[d, k - 1, c], (right, left)[d])

    def back(d, k, c):
        rows = pl.ds(HALF * c, HALF)
        return remote(
            back_out.at[d, k - 1, rows],
            back_in.at[d, k - 1, rows],
            back_s.at[d, k - 1, c],
            back_r.at[d, k - 1, c],
            (left, right)[d],
        )

    def hid_copy(tower, o, wait=False):
        index = ((x - o + 4) % 4) * 2 + core if wait else q
        return remote(
            hx.at[tower, index],
            hx.at[tower, index],
            hid_s.at[tower, o - 1],
            hid_r.at[tower, o - 1],
            place(x=(x + o) % NX),
        )

    def relay(tower, o, wait=False):
        index = ((x - o + 4) % 4) * 2 + ((1 - core) if wait else core)
        return remote(
            hx.at[tower, index], hx.at[tower, index], rel_s.at[tower, o], rel_r.at[tower, o], sibling
        )

    loads[0].wait()
    loads[1].wait()
    tt[0, pl.ds(0, TOK)] = project(TEXT)
    pl.semaphore_wait(barrier, 32)
    for c in (0, 1):
        ring(0, 1, c).start()
        ring(1, 1, 1 - c).start()
    loads[2].wait()
    loads[3].wait()
    emb[pl.ds(0, TOK)] = project(CLIP)
    share_emb = remote(
        emb.at[pl.ds(0, TOK)], emb.at[pl.ds(TOK, TOK)], share_s.at[0], share_r.at[0], partner
    )
    share_emb.start()
    for tower in (CLIP, TEXT):
        for o in (1, 3, 2):
            hid_copy(tower, o).start()
        relay(tower, 0).start()

    scale = scale_ref[0]
    shift = shift_ref[0]

    def work(k, rows):
        base0 = (yl * NZ + (z - k + NZ) % NZ) * TOK
        base1 = (yl * NZ + (z + k) % NZ) * TOK
        t = tt[k, pl.ds(0, rows)]
        a = emb[...]
        scores = scale * lax.dot_general(
            t, a, (((1,), (1,)), ((), ())), preferred_element_type=F32
        ) + shift
        row = lax.broadcasted_iota(jnp.int32, (rows, 2 * TOK), 0)
        place_of = jnp.where(row < TOK, base0 + row, base1 + row - TOK)
        wanted = jnp.concatenate(
            [match_ref[pl.ds(blk, 1), :], match_ref[pl.ds((1 - yl) * NZ + z, 1), :]], axis=1
        )
        hit = place_of == wanted
        flipped = jnp.where(hit, scores, -scores)
        coef = (jnp.where(hit, -scale, scale) / (1.0 + jnp.exp(flipped))).astype(BF16)
        part[k, pl.ds(0, rows)] = jnp.dot(coef, a, preferred_element_type=F32)
        return lax.dot_general(coef, t, (((0,), (0,)), ((), ())), preferred_element_type=F32)

    share_emb.wait_recv()
    cacc[...] = work(0, TOK)

    @pl.loop(1, 7)
    def _(k):
        for c in (0, 1):
            for d in (0, 1):
                cc = c if d == 0 else 1 - c
                ring_k(ring, d, k, cc)
        cacc[...] += work(k, 2 * TOK)

    def last_wait(d, k, c):
        ring(d, k, c).wait_recv()

    for d in (0, 1):
        last_wait(d, 7, d)
        ring(d, 8, d).start()
    for d in (0, 1):
        last_wait(d, 7, 1 - d)
    cacc[...] += work(7, 2 * TOK)

    def run(d, k, c):
        return part[k, pl.ds((0 if k == 8 else TOK * d) + HALF * c, HALF)]

    def send_fresh(d, k, c):
        back_out[d, k - 1, pl.ds(HALF * c, HALF)] = run(d, k, c).astype(BF16)
        back(d, k, c).start()

    def send_sum(d, k, c):
        rows = pl.ds(HALF * c, HALF)
        back(d, k + 1, c).wait_recv()
        back_out[d, k - 1, rows] = (run(d, k, c) + back_in[d, k, rows].astype(F32)).astype(BF16)
        back(d, k, c).start()

    for d in (0, 1):
        send_fresh(d, 7, 1 - d)
    for d in (0, 1):
        last_wait(d, 8, d)
    cacc[...] += work(8, TOK)
    for d in (0, 1):
        send_fresh(d, 8, d)

    share_out[...] = cacc[pl.ds(TOK, TOK)].astype(BF16)
    share_grad = remote(share_out, share_in, share_s.at[1], share_r.at[1], partner)
    share_grad.start()

    def ga_copy(tower, o, wait=False):
        to = (q + o) % 8
        slot = (q - o + 8) % 8 if wait else q
        return remote(
            g_out.at[tower, to],
            g_in.at[tower, slot],
            ga_s.at[tower, o - 1],
            ga_r.at[tower, o - 1],
            place(x=to // 2, core=to % 2),
        )

    def yb_copy(tower, o):
        to = (y + o) % 4
        return remote(
            y_out.at[tower, to],
            y_in.at[tower, o],
            yb_s.at[tower, o - 1],
            yb_r.at[tower, o - 1],
            place(y=to),
        )

    def zc_copy(tower, o):
        to = (z + o) % NZ
        return remote(
            z_out.at[tower, to],
            z_in.at[tower, o],
            zc_s.at[tower, o - 1],
            zc_r.at[tower, o - 1],
            place(z=to),
        )

    def fd_copy(tower, o, wait=False):
        to = (grp + o) % 16
        slot = (grp - o + 16) % 16 if wait else grp
        return remote(
            f_all.at[tower, slot if wait else grp],
            f_all.at[tower, slot],
            fd_s.at[tower, o - 1],
            fd_r.at[tower, o - 1],
            (to, blk),
        )

    def raw_grad(tower, grad):
        vec = unit[tower]
        radial = jnp.sum(vec * grad, axis=1, keepdims=True)
        raw = ((grad - vec * radial) / length[tower]).astype(BF16)
        for j in range(8):
            g_out[tower, j] = raw[:, 128 * j : 128 * (j + 1)]

        @pl.loop(1, 8)
        def _(o):
            ga_copy(tower, o).start()

        return raw

    def hidden_grad(tower, raw, out):
        out[...] = lax.dot_general(
            raw, w[tower], (((1,), (1,)), ((), ())), preferred_element_type=F32
        ).astype(BF16)

    def turn(tower, first, count):
        for j in range(first, first + count):
            ht[tower, :, pl.ds(128 * j, 128)] = hx[tower, j].T

    def weight(tower):
        g_in[tower, q] = g_out[tower, q]

        @pl.loop(1, 8)
        def _(o):
            ga_copy(tower, o, True).wait_recv()

        g = g_in[tower].reshape(8 * TOK, 128)
        for yl_to in (0, 1):
            term = jnp.dot(
                ht[tower, pl.ds(512 * yl_to, 512), :], g, preferred_element_type=F32
            ).reshape(NZ, 2, 16, 128).astype(BF16)
            for yh_to in (0, 1):
                y_out[tower, yh_to * 2 + yl_to] = term[:, yh_to]

        @pl.loop(1, 4)
        def _(o):
            yb_copy(tower, o).start()

    def over_y(tower):
        total = y_out[tower, y].astype(F32)
        for o in range(1, 4):
            yb_copy(tower, o).wait_recv()
            total = total + y_in[tower, o].astype(F32)
        z_out[tower] = total.astype(BF16)

        @pl.loop(1, NZ)
        def _(o):
            zc_copy(tower, o).start()

    def over_z(tower):
        @pl.loop(1, NZ)
        def _(o):
            zc_copy(tower, o).wait_recv()

        z_in[tower, 0] = z_out[tower, z]
        f_all[tower, grp] = jnp.sum(z_in[tower].astype(F32), axis=0)

        @pl.loop(1, 16)
        def _(o):
            fd_copy(tower, o).start()

    def finish(tower, out):
        @pl.loop(1, 16)
        def _(o):
            fd_copy(tower, o, True).wait_recv()

        for yh_from in (0, 1):
            for j in range(8):
                out[pl.ds(16 * yh_from, 16), pl.ds(128 * j, 128)] = f_all[tower, 8 * yh_from + j]

    def relays(tower):
        for o in (1, 2, 3):
            hid_copy(tower, o, True).wait_recv()
            relay(tower, o).start()

    def relays_done(tower):
        for o in range(4):
            relay(tower, o, True).wait_recv()

    def clip_back():
        share_grad.wait_recv()
        grad = cacc[pl.ds(0, TOK)] + share_in[...].astype(F32)
        hidden_grad(CLIP, raw_grad(CLIP, grad), clip_hid)

    def stage(j):
        if j == 6:
            relays(CLIP)
        elif j == 5:
            relays_done(CLIP)
            clip_back()
        elif j == 4:
            turn(CLIP, 0, 8)
        elif j == 3:
            weight(CLIP)
            relays(TEXT)
        elif j == 2:
            over_y(CLIP)
            relays_done(TEXT)
            turn(TEXT, 0, 4)
        elif j == 1:
            over_z(CLIP)
            turn(TEXT, 4, 4)
        else:
            finish(CLIP, clip_wg)

    for j in range(6, -1, -1):
        for d in (0, 1):
            if j >= 1:
                send_sum(d, j, 1 - d)
            else:
                back(d, 1, 1 - d).wait_recv()
        for d in (0, 1):
            send_sum(d, j + 1, d)
        stage(j)
    for d in (0, 1):
        back(d, 1, d).wait_recv()

    grad = part[0, pl.ds(0, TOK)] + back_in[0, 0].astype(F32) + back_in[1, 0].astype(F32)
    raw = raw_grad(TEXT, grad)
    hidden_grad(TEXT, raw, text_hid)
    weight(TEXT)
    over_y(TEXT)
    over_z(TEXT)
    finish(TEXT, text_wg)

    share_emb.wait_send()
    share_grad.wait_send()
    for d in (0, 1):
        for c in (0, 1):
            ring(d, 1, c).wait_send()

            @pl.loop(2, 8)
            def _(k):
                ring(d, k, c).wait_send()

            @pl.loop(1, 8)
            def _(k):
                back(d, k, c).wait_send()

        ring(d, 8, d).wait_send()
        back(d, 8, d).wait_send()
    for tower in (CLIP, TEXT):
        for o in range(4):
            relay(tower, o).wait_send()
        for o in (1, 2, 3):
            hid_copy(tower, o).wait_send()
            yb_copy(tower, o).wait_send()

        @pl.loop(1, 8)
        def _(o):
            ga_copy(tower, o).wait_send()

        @pl.loop(1, 16)
        def _(o):
            zc_copy(tower, o).wait_send()
            fd_copy(tower, o).wait_send()


def ring_k(ring, d, k, c):
    ring(d, k, c).wait_recv()
    ring(d, k + 1, c).start()


def local(hv, hc, wv, wc, match, multiplier, offset):
    vmem = pl.BlockSpec(memory_space=pltpu.VMEM)
    smem = pl.BlockSpec(memory_space=pltpu.SMEM)
    anywhere = pl.BlockSpec(memory_space=pl.ANY)
    dma = pltpu.SemaphoreType.DMA
    return pl.pallas_call(
        kernel,
        out_shape=(
            jax.ShapeDtypeStruct((TOK, D), BF16),
            jax.ShapeDtypeStruct((TOK, D), BF16),
            jax.ShapeDtypeStruct((32, E), F32),
            jax.ShapeDtypeStruct((32, E), F32),
        ),
        in_specs=[anywhere] * 4 + [vmem, smem, smem],
        out_specs=(vmem,) * 4,
        scratch_shapes=[
            pltpu.VMEM((2, D, E), BF16),
            pltpu.VMEM((2, 8, TOK, D), BF16),
            pltpu.VMEM((2, D, 8 * TOK), BF16),
            pltpu.VMEM((2, TOK, E), F32),
            pltpu.VMEM((2, TOK, 1), F32),
            pltpu.VMEM((9, 2 * TOK, E), BF16),
            pltpu.VMEM((2 * TOK, E), BF16),
            pltpu.VMEM((9, 2 * TOK, E), F32),
            pltpu.VMEM((2 * TOK, E), F32),
            pltpu.VMEM((2, 8, TOK, E), BF16),
            pltpu.VMEM((2, 8, TOK, E), BF16),
            pltpu.VMEM((TOK, E), BF16),
            pltpu.VMEM((TOK, E), BF16),
            pltpu.VMEM((2, 8, TOK, 128), BF16),
            pltpu.VMEM((2, 8, TOK, 128), BF16),
            pltpu.VMEM((2, 4, NZ, 16, 128), BF16),
            pltpu.VMEM((2, 4, NZ, 16, 128), BF16),
            pltpu.VMEM((2, NZ, 16, 128), BF16),
            pltpu.VMEM((2, NZ, 16, 128), BF16),
            pltpu.VMEM((2, 16, 16, 128), F32),
            dma((4,)),
            dma((2, 8, 2)),
            dma((2, 8, 2)),
            dma((2, 8, 2)),
            dma((2, 8, 2)),
            dma((2,)),
            dma((2,)),
            dma((2, 3)),
            dma((2, 3)),
            dma((2, 4)),
            dma((2, 4)),
            dma((2, 7)),
            dma((2, 7)),
            dma((2, 3)),
            dma((2, 3)),
            dma((2, 15)),
            dma((2, 15)),
            dma((2, 15)),
            dma((2, 15)),
        ],
        compiler_params=pltpu.CompilerParams(
            collective_id=0, has_side_effects=True, vmem_limit_bytes=60 << 20
        ),
    )(hv, hc, wv, wc, match.reshape(32, TOK), multiplier, offset)


def solution(mesh):
    placed = (P(("grp", "blk"), None), P(("grp", "blk"), None), P(), P(), P("grp"), P(), P())
    return jax.shard_map(
        local,
        mesh=mesh,
        in_specs=placed,
        out_specs=(
            P(("grp", "blk"), None),
            P(("grp", "blk"), None),
            P("blk", None),
            P("blk", None),
        ),
        check_vma=False,
    )
```

time: 737 us -> 151 us (0.20)
  waiting for transfers between devices: 664 us -> 0 us
  Pallas kernels: 0 us -> 142 us
  matrix products: 38.9 us -> 0 us
  between operations: 15.1 us -> 1.93 us
  local copies, waits for them, and re-layouts: 16.3 us -> 6.47 us
    all_gather x2 -> x0, waiting for transfers between devices: 256 us -> none  [the longest x1 130 us: local(): video_slice = lax.all_gather(video_vector, 'blk', axis=0, tiled=True)]
    unnamed x7 -> x0, waiting for transfers between devices: 242 us -> none
    psum x1 -> x0, waiting for transfers between devices: 166 us -> none  [local(): lax.psum(shards[0].astype(jnp.bfloat16), 'grp').astype(jnp.float32)]
    pallas_call x0 -> x1, Pallas kernels: none -> 142 us  [local(): pl.pallas_call(kernel, out_shape=(jax.ShapeDtypeStruct((TOK, D), BF16), j...]
    dot_general x8 -> x0, matrix products: 38.9 us -> none  [the longest x3 18.5 us: transposed_product(): lax.dot_general(coef_block, emb_block, (((0,), (0,)), ((), ())), preferre...]
    unnamed x14 -> x4, local copies, waits for them, and re-layouts: 16.2 us -> 6.47 us
  transfers between devices with their start and end apart: 5 -> 0, of which waited for: 5 -> 0; matrix products, arithmetic and copies ran while one was open for 7% -> 0% of each run, Pallas kernels for 0% -> 0%
where the time goes in v1:
time: 151 us; the launch traced here: 150 us
  Pallas kernels  142 us (94%)
  local copies, waits for them, and re-layouts  6.47 us (4%)
  between operations  1.93 us (1%)
    pallas_call x1, Pallas kernels, local(): pl.pallas_call(kernel, out_shape=(jax.ShapeDtypeStruct((TOK, D), BF16), j...  142 us
    unnamed x4, local copies, waits for them, and re-layouts  6.47 us

profile of v1, /device:TPU:1, one launch (start us, length us, event | category | flops | bytes accessed | tf_op | source)
XLA Modules:
  0.0 150.4 jit_solution(13825292396375853128)
XLA Ops:
  1.9 142.0 %shard_map.102 = (bf16[128,1024]{1,0:T(8,128)(2,1)}, bf16[128,1024]{1,0:T(8,128)(2,1)}, f32[32,1024]{1,0:T(8,128)}, f32[32,1024]{1,0:T(8,128)}) custom-call(bf16[128,1024]{1,0:T(8,128)(2,1)} %hv_hbm.1, bf16[128,1024]{1,0:T(8,128)(2,1)} %hc_hbm.1, bf16[1024,1024]{1,0:T(8,128)(2,1)} %wv_hbm.1, bf16[1024,1024]{1,0:T(8,128)(2,1)} %wc_hbm.1, s32[32,128]{1,0:T(8,128)} %bitcast.1, ...), custom_call_target="tpu_custom_call" | custom-call | tf_op jit(solution)/shard_map/pallas_call | solution.py:445
  144.0 1.7 %copy.17 = bf16[128,1024]{1,0:T(8,128)(2,1)} copy(bf16[128,1024]{1,0:T(8,128)(2,1)} %get-tuple-element.8) | data formatting | bytes 524288
  145.6 1.7 %copy.18 = bf16[128,1024]{1,0:T(8,128)(2,1)} copy(bf16[128,1024]{1,0:T(8,128)(2,1)} %get-tuple-element.9) | data formatting | bytes 524288
  147.3 1.6 %copy.19 = f32[32,1024]{1,0:T(8,128)} copy(f32[32,1024]{1,0:T(8,128)} %get-tuple-element.10) | data formatting | bytes 262144
  148.9 1.6 %copy.20 = f32[32,1024]{1,0:T(8,128)} copy(f32[32,1024]{1,0:T(8,128)} %get-tuple-element.11) | data formatting | bytes 262144

commit v2 on v1

v2 whole, which is shorter than its diff:
```python
import jax
import jax.numpy as jnp
from jax import lax
from jax.experimental import pallas as pl
from jax.experimental.pallas import tpu as pltpu
from jax.sharding import PartitionSpec as P

MESH = pl.DeviceIdType.MESH
F32 = jnp.float32
BF16 = jnp.bfloat16
NX, NZ, TOK, D, E = 4, 16, 128, 1024, 1024
NC = 4
ROWS = TOK // NC
LATE = ((0, 1), (2, 3))
AHEAD = ((2, 3), (0, 1))
CLIP, TEXT = 0, 1


def kernel(
    hv_hbm,
    hc_hbm,
    wv_hbm,
    wc_hbm,
    match_ref,
    scale_ref,
    shift_ref,
    clip_hid,
    text_hid,
    clip_wg,
    text_wg,
    w,
    hx,
    ht,
    unit,
    length,
    tt,
    emb,
    part,
    cacc,
    back_in,
    back_out,
    share_out,
    share_in,
    g_out,
    g_in,
    y_out,
    y_in,
    z_out,
    z_in,
    f_in,
    hid_out,
    wg_out,
    load_sem,
    out_sem,
    ring_s,
    ring_r,
    back_s,
    back_r,
    share_s,
    share_r,
    hid_s,
    hid_r,
    rel_s,
    rel_r,
    ga_s,
    ga_r,
    yb_s,
    yb_r,
    zc_s,
    zc_r,
    fd_s,
    fd_r,
):
    grp = lax.axis_index("grp")
    blk = lax.axis_index("blk")
    yh, x, core = grp // 8, (grp // 2) % 4, grp % 2
    yl, z = blk // NZ, blk % NZ
    y = yh * 2 + yl
    q = x * 2 + core

    def place(x=x, y=y, z=z, core=core):
        return ((y // 2) * 8 + x * 2 + core, (y % 2) * NZ + z)

    right, left = place(z=(z + 1) % NZ), place(z=(z + NZ - 1) % NZ)
    partner = place(y=yh * 2 + 1 - yl)
    sibling = place(core=1 - core)

    def remote(src, dst, s, r, device):
        return pltpu.make_async_remote_copy(
            src_ref=src, dst_ref=dst, send_sem=s, recv_sem=r, device_id=device, device_id_type=MESH
        )

    loads = [
        pltpu.make_async_copy(wc_hbm, w.at[TEXT], load_sem.at[0]),
        pltpu.make_async_copy(hc_hbm, hx.at[TEXT, q], load_sem.at[1]),
        pltpu.make_async_copy(wv_hbm, w.at[CLIP], load_sem.at[2]),
        pltpu.make_async_copy(hv_hbm, hx.at[CLIP, q], load_sem.at[3]),
    ]
    for copy in loads:
        copy.start()

    barrier = pltpu.get_barrier_semaphore()
    near = [right, left, sibling]
    near += [place(x=(x + o) % 4) for o in (1, 2, 3)] + [place(y=(y + o) % 4) for o in (1, 2, 3)]
    for device in near:
        pl.semaphore_signal(barrier, 1, device_id=device, device_id_type=MESH)

    def project(tower):
        raw = jnp.dot(hx[tower, q], w[tower], preferred_element_type=F32)
        size = jnp.sqrt(jnp.sum(raw * raw, axis=1, keepdims=True) + 1e-06)
        vec = raw / size
        unit[tower] = vec
        length[tower] = size
        return vec.astype(BF16)

    def ring(d, k, c):
        first = isinstance(k, int) and k == 1
        last = isinstance(k, int) and k == 8
        src = tt.at[k - 1, pl.ds((0 if first else TOK * d) + ROWS * c, ROWS)]
        dst = tt.at[k, pl.ds((0 if last else TOK * d) + ROWS * c, ROWS)]
        return remote(src, dst, ring_s.at[d, k - 1, c], ring_r.at[d, k - 1, c], (right, left)[d])

    def back(d, k, c):
        rows = pl.ds(ROWS * c, ROWS)
        return remote(
            back_out.at[d, k - 1, rows],
            back_in.at[d, k - 1, rows],
            back_s.at[d, k - 1, c],
            back_r.at[d, k - 1, c],
            (left, right)[d],
        )

    def hid_copy(tower, o, wait=False):
        index = ((x - o + 4) % 4) * 2 + core if wait else q
        return remote(
            hx.at[tower, index],
            hx.at[tower, index],
            hid_s.at[tower, o - 1],
            hid_r.at[tower, o - 1],
            place(x=(x + o) % NX),
        )

    def relay(tower, o, wait=False):
        index = ((x - o + 4) % 4) * 2 + ((1 - core) if wait else core)
        return remote(
            hx.at[tower, index], hx.at[tower, index], rel_s.at[tower, o], rel_r.at[tower, o], sibling
        )

    loads[0].wait()
    loads[1].wait()
    tt[0, pl.ds(0, TOK)] = project(TEXT)
    pl.semaphore_wait(barrier, len(near))
    for i in range(NC):
        for d in (0, 1):
            ring(d, 1, (LATE[d] + AHEAD[d])[i]).start()
    loads[2].wait()
    loads[3].wait()
    emb[pl.ds(0, TOK)] = project(CLIP)
    share_emb = remote(
        emb.at[pl.ds(0, TOK)], emb.at[pl.ds(TOK, TOK)], share_s.at[0], share_r.at[0], partner
    )
    share_emb.start()
    for tower in (CLIP, TEXT):
        for o in (1, 3, 2):
            hid_copy(tower, o).start()
        relay(tower, 0).start()

    scale = scale_ref[0]
    shift = shift_ref[0]

    def work(k, rows):
        base0 = (yl * NZ + (z - k + NZ) % NZ) * TOK
        base1 = (yl * NZ + (z + k) % NZ) * TOK
        t = tt[k, pl.ds(0, rows)]
        a = emb[...]
        scores = scale * lax.dot_general(
            t, a, (((1,), (1,)), ((), ())), preferred_element_type=F32
        ) + shift
        row = lax.broadcasted_iota(jnp.int32, (rows, 2 * TOK), 0)
        place_of = jnp.where(row < TOK, base0 + row, base1 + row - TOK)
        wanted = jnp.concatenate(
            [match_ref[pl.ds(blk, 1), :], match_ref[pl.ds((1 - yl) * NZ + z, 1), :]], axis=1
        )
        hit = place_of == wanted
        flipped = jnp.where(hit, scores, -scores)
        coef = (jnp.where(hit, -scale, scale) / (1.0 + jnp.exp(flipped))).astype(BF16)
        part[k, pl.ds(0, rows)] = jnp.dot(coef, a, preferred_element_type=F32)
        return lax.dot_general(coef, t, (((0,), (0,)), ((), ())), preferred_element_type=F32)

    def forward(k):
        for i in range(NC):
            for d in (0, 1):
                c = (LATE[d] + AHEAD[d])[i]
                ring(d, k, c).wait_recv()
                if not (isinstance(k, int) and k == 7 and c in AHEAD[d]):
                    ring(d, k + 1, c).start()

    forward(1)
    share_emb.wait_recv()
    cacc[...] = work(0, TOK)

    @pl.loop(2, 7)
    def _(k):
        forward(k)
        cacc[...] += work(k - 1, 2 * TOK)

    def run(d, k, c):
        return part[k, pl.ds((0 if k == 8 else TOK * d) + ROWS * c, ROWS)]

    def send_fresh(d, k, c):
        back_out[d, k - 1, pl.ds(ROWS * c, ROWS)] = run(d, k, c).astype(BF16)
        back(d, k, c).start()

    def send_sum(d, k, c):
        rows = pl.ds(ROWS * c, ROWS)
        back(d, k + 1, c).wait_recv()
        back_out[d, k - 1, rows] = (run(d, k, c) + back_in[d, k, rows].astype(F32)).astype(BF16)
        back(d, k, c).start()

    forward(7)

    @pl.loop(6, 8)
    def _(k):
        cacc[...] += work(k, 2 * TOK)

    for i in (0, 1):
        for d in (0, 1):
            send_fresh(d, 7, AHEAD[d][i])
    for i in (0, 1):
        for d in (0, 1):
            ring(d, 8, LATE[d][i]).wait_recv()
    cacc[...] += work(8, TOK)
    for i in (0, 1):
        for d in (0, 1):
            send_fresh(d, 8, LATE[d][i])

    share_out[...] = cacc[pl.ds(TOK, TOK)].astype(BF16)
    share_grad = remote(share_out, share_in, share_s.at[1], share_r.at[1], partner)
    share_grad.start()

    def ga_copy(tower, o, wait=False):
        to = (q + o) % 8
        return remote(
            g_out.at[tower, to],
            g_in.at[tower, (q - o + 8) % 8 if wait else q],
            ga_s.at[tower, o - 1],
            ga_r.at[tower, o - 1],
            place(x=to // 2, core=to % 2),
        )

    def yb_copy(tower, o):
        to = (y + o) % 4
        return remote(
            y_out.at[tower, to],
            y_in.at[tower, o],
            yb_s.at[tower, o - 1],
            yb_r.at[tower, o - 1],
            place(y=to),
        )

    def zc_copy(tower, o):
        to = (z + o) % NZ
        return remote(
            z_out.at[tower, to], z_in.at[tower, o], zc_s.at[tower], zc_r.at[tower], place(z=to)
        )

    def zc_all(tower):
        rest = pl.ds(1, NZ - 1)
        return remote(
            z_out.at[tower, rest], z_in.at[tower, rest], zc_s.at[tower], zc_r.at[tower], right
        )

    def fd_copy(tower, o):
        return remote(
            f_in.at[tower, 0],
            f_in.at[tower, o],
            fd_s.at[tower],
            fd_r.at[tower],
            ((grp + o) % 16, blk),
        )

    def fd_all(tower):
        rest = pl.ds(1, 15)
        return remote(
            f_in.at[tower, rest], f_in.at[tower, rest], fd_s.at[tower], fd_r.at[tower], right
        )

    def raw_grad(tower, grad):
        vec = unit[tower]
        radial = jnp.sum(vec * grad, axis=1, keepdims=True)
        raw = ((grad - vec * radial) / length[tower]).astype(BF16)
        for j in range(8):
            g_out[tower, j] = raw[:, 128 * j : 128 * (j + 1)]

        @pl.loop(1, 8)
        def _(o):
            ga_copy(tower, o).start()

    def hidden_copy(tower):
        return pltpu.make_async_copy(
            hid_out.at[tower], (clip_hid, text_hid)[tower], out_sem.at[tower]
        )

    def hidden_grad(tower):
        raw = jnp.concatenate([g_out[tower, j] for j in range(8)], axis=1)
        hid_out[tower] = lax.dot_general(
            raw, w[tower], (((1,), (1,)), ((), ())), preferred_element_type=F32
        ).astype(BF16)
        hidden_copy(tower).start()

    def turn(tower, *blocks):
        for j in blocks:
            ht[tower, :, pl.ds(128 * j, 128)] = hx[tower, j].T

    def gathered(tower):
        g_in[tower, q] = g_out[tower, q]

        @pl.loop(1, 8)
        def _(o):
            ga_copy(tower, o, True).wait_recv()

    def weight(tower, own):
        to = yl if own else 1 - yl
        g = g_in[tower].reshape(8 * TOK, 128)
        rows = pl.ds(pl.multiple_of(512 * to, 512), 512)
        term = jnp.dot(ht[tower, rows, :], g, preferred_element_type=F32)
        term = term.reshape(NZ, 2, 16, 128).astype(BF16)
        for yh_to in (0, 1):
            y_out[tower, yh_to * 2 + to] = term[:, yh_to]
        for o in (2,) if own else (1, 3):
            yb_copy(tower, o).start()

    def over_y(tower):
        total = y_out[tower, y].astype(F32)
        for o in (1, 3, 2):
            yb_copy(tower, o).wait_recv()
            total = total + y_in[tower, o].astype(F32)
        z_out[tower] = total.astype(BF16)

    def send_z(tower):
        for o in (8, 7, 9, 6, 10, 5, 11, 4, 12, 3, 13, 2, 14, 1, 15):
            zc_copy(tower, o).start()

    def over_z(tower):
        z_in[tower, 0] = z_out[tower, z]
        zc_all(tower).wait_recv()
        f_in[tower, 0] = jnp.sum(z_in[tower].astype(F32), axis=0).astype(BF16)
        for o in range(1, 16):
            fd_copy(tower, o).start()

    def weight_copy(tower):
        return pltpu.make_async_copy(
            wg_out.at[tower], (clip_wg, text_wg)[tower], out_sem.at[2 + tower]
        )

    def finish(tower):
        fd_all(tower).wait_recv()
        for j in range(16):
            piece = f_in[tower, (grp - j + 16) % 16].astype(F32)
            wg_out[tower, pl.ds(16 * (j // 8), 16), pl.ds(128 * (j % 8), 128)] = piece
        weight_copy(tower).start()

    def relays(tower):
        for o in (1, 2, 3):
            hid_copy(tower, o, True).wait_recv()
            relay(tower, o).start()

    def relays_done(tower):
        for o in range(4):
            relay(tower, o, True).wait_recv()

    def clip_raw():
        share_grad.wait_recv()
        raw_grad(CLIP, cacc[pl.ds(0, TOK)] + share_in[...].astype(F32))

    def ring_left(k):
        for d in (0, 1):
            for c in range(NC) if k < 8 else LATE[d]:
                ring(d, k, c).wait_send()

    def hidden_left():
        for tower in (CLIP, TEXT):
            for o in range(4):
                relay(tower, o).wait_send()
            for o in (1, 2, 3):
                hid_copy(tower, o).wait_send()

    def columns_left(tower):
        @pl.loop(1, 8)
        def _(o):
            ga_copy(tower, o).wait_send()

    def sums_left(tower):
        for o in (1, 2, 3):
            yb_copy(tower, o).wait_send()

    pieces = {
        0: lambda: relays(CLIP),
        2: lambda: ring_left(1),
        3: lambda: relays_done(CLIP),
        4: lambda: turn(CLIP, 0, 1),
        5: lambda: turn(CLIP, 2, 3),
        6: lambda: clip_raw(),
        7: lambda: hidden_grad(CLIP),
        8: lambda: turn(CLIP, 4, 5),
        9: lambda: turn(CLIP, 6, 7),
        10: lambda: relays(TEXT),
        11: lambda: gathered(CLIP),
        12: lambda: weight(CLIP, False),
        13: lambda: weight(CLIP, True),
        14: lambda: relays_done(TEXT),
        15: lambda: turn(TEXT, 0, 1),
        16: lambda: turn(TEXT, 2, 3),
        17: lambda: turn(TEXT, 4, 5),
        18: lambda: turn(TEXT, 6, 7),
        19: lambda: over_y(CLIP),
        20: lambda: ring_left(2),
        21: lambda: ring_left(3),
        22: lambda: ring_left(4),
        23: lambda: ring_left(5),
        24: lambda: ring_left(6),
        25: lambda: ring_left(7),
        26: lambda: ring_left(8),
    }
    for j in range(6, -1, -1):
        for i in range(4):
            for d in (0, 1):
                if i >= 2:
                    send_sum(d, j + 1, LATE[d][i - 2])
                elif j >= 1:
                    send_sum(d, j, AHEAD[d][i])
                else:
                    back(d, 1, AHEAD[d][i]).wait_recv()
            pieces.get((6 - j) * 4 + i, lambda: None)()
    for i in (0, 1):
        for d in (0, 1):
            back(d, 1, LATE[d][i]).wait_recv()

    grad = part[0, pl.ds(0, TOK)] + back_in[0, 0].astype(F32) + back_in[1, 0].astype(F32)
    raw_grad(TEXT, grad)
    send_z(CLIP)
    hidden_grad(TEXT)
    gathered(TEXT)
    weight(TEXT, False)
    weight(TEXT, True)
    over_z(CLIP)
    over_y(TEXT)
    send_z(TEXT)
    for d in (0, 1):
        for c in range(NC):

            @pl.loop(1, 8)
            def _(k):
                back(d, k, c).wait_send()

        for c in LATE[d]:
            back(d, 8, c).wait_send()
    finish(CLIP)
    hidden_left()
    over_z(TEXT)
    share_emb.wait_send()
    share_grad.wait_send()
    for tower in (CLIP, TEXT):
        columns_left(tower)
        sums_left(tower)
        zc_all(tower).wait_send()
    fd_all(CLIP).wait_send()
    hidden_copy(CLIP).wait()
    hidden_copy(TEXT).wait()
    weight_copy(CLIP).wait()
    finish(TEXT)
    fd_all(TEXT).wait_send()
    weight_copy(TEXT).wait()


def hand_over(*refs):
    for i in range(4):
        refs[4 + i][...] = refs[i][...]


def local(hv, hc, wv, wc, match, multiplier, offset):
    vmem = pl.BlockSpec(memory_space=pltpu.VMEM)
    smem = pl.BlockSpec(memory_space=pltpu.SMEM)
    anywhere = pl.BlockSpec(memory_space=pl.ANY)
    dma = pltpu.SemaphoreType.DMA
    shapes = (
        jax.ShapeDtypeStruct((TOK, D), BF16),
        jax.ShapeDtypeStruct((TOK, D), BF16),
        jax.ShapeDtypeStruct((32, E), F32),
        jax.ShapeDtypeStruct((32, E), F32),
    )
    results = pl.pallas_call(
        kernel,
        out_shape=shapes,
        in_specs=[anywhere] * 4 + [vmem, smem, smem],
        out_specs=(anywhere,) * 4,
        scratch_shapes=[
            pltpu.VMEM((2, D, E), BF16),
            pltpu.VMEM((2, 8, TOK, D), BF16),
            pltpu.VMEM((2, D, 8 * TOK), BF16),
            pltpu.VMEM((2, TOK, E), F32),
            pltpu.VMEM((2, TOK, 1), F32),
            pltpu.VMEM((9, 2 * TOK, E), BF16),
            pltpu.VMEM((2 * TOK, E), BF16),
            pltpu.VMEM((9, 2 * TOK, E), F32),
            pltpu.VMEM((2 * TOK, E), F32),
            pltpu.VMEM((2, 8, TOK, E), BF16),
            pltpu.VMEM((2, 8, TOK, E), BF16),
            pltpu.VMEM((TOK, E), BF16),
            pltpu.VMEM((TOK, E), BF16),
            pltpu.VMEM((2, 8, TOK, 128), BF16),
            pltpu.VMEM((2, 8, TOK, 128), BF16),
            pltpu.VMEM((2, 4, NZ, 16, 128), BF16),
            pltpu.VMEM((2, 4, NZ, 16, 128), BF16),
            pltpu.VMEM((2, NZ, 16, 128), BF16),
            pltpu.VMEM((2, NZ, 16, 128), BF16),
            pltpu.VMEM((2, 16, 16, 128), BF16),
            pltpu.VMEM((2, TOK, D), BF16),
            pltpu.VMEM((2, 32, E), F32),
            dma((4,)),
            dma((4,)),
            dma((2, 8, NC)),
            dma((2, 8, NC)),
            dma((2, 8, NC)),
            dma((2, 8, NC)),
            dma((2,)),
            dma((2,)),
            dma((2, 3)),
            dma((2, 3)),
            dma((2, 4)),
            dma((2, 4)),
            dma((2, 7)),
            dma((2, 7)),
            dma((2, 3)),
            dma((2, 3)),
            dma((2,)),
            dma((2,)),
            dma((2,)),
            dma((2,)),
        ],
        compiler_params=pltpu.CompilerParams(
            collective_id=0, has_side_effects=True, vmem_limit_bytes=60 << 20
        ),
    )(hv, hc, wv, wc, match.reshape(32, TOK), multiplier, offset)
    return pl.pallas_call(
        hand_over,
        out_shape=shapes,
        in_specs=[vmem] * 4,
        out_specs=(vmem,) * 4,
    )(*results)


def solution(mesh):
    placed = (P(("grp", "blk"), None), P(("grp", "blk"), None), P(), P(), P("grp"), P(), P())
    return jax.shard_map(
        local,
        mesh=mesh,
        in_specs=placed,
        out_specs=(
            P(("grp", "blk"), None),
            P(("grp", "blk"), None),
            P("blk", None),
            P("blk", None),
        ),
        check_vma=False,
    )
```

time: 151 us -> 136 us (0.901)
  Pallas kernels: 142 us -> 134 us
  local copies, waits for them, and re-layouts: 6.47 us -> 0 us
    pallas_call x1 -> x2, Pallas kernels: 142 us -> 134 us  [the longest x1 132 us: local(): pl.pallas_call(kernel, out_shape=shapes, in_specs=[anywhere] * 4 + [vmem,...]
    unnamed x4 -> x0, local copies, waits for them, and re-layouts: 6.47 us -> none
where the time goes in v2:
time: 136 us
  Pallas kernels  134 us (99%)
  between operations  1.93 us (1%)
    pallas_call x1, Pallas kernels, local(): pl.pallas_call(kernel, out_shape=shapes, in_specs=[anywhere] * 4 + [vmem,...  132 us

profile of v2, /device:TPU:1, one launch (start us, length us, event | category | flops | bytes accessed | tf_op | source)
XLA Modules:
  0.0 136.2 jit_solution(651480784108858376)
XLA Ops:
  1.9 132.2 %shard_map.102 = (bf16[128,1024]{1,0:T(8,128)(2,1)}, bf16[128,1024]{1,0:T(8,128)(2,1)}, f32[32,1024]{1,0:T(8,128)}, f32[32,1024]{1,0:T(8,128)}) custom-call(bf16[128,1024]{1,0:T(8,128)(2,1)} %hv_hbm.1, bf16[128,1024]{1,0:T(8,128)(2,1)} %hc_hbm.1, bf16[1024,1024]{1,0:T(8,128)(2,1)} %wv_hbm.1, bf16[1024,1024]{1,0:T(8,128)(2,1)} %wc_hbm.1, s32[32,128]{1,0:T(8,128)} %bitcast.1, ...), custom_call_target="tpu_custom_call" | custom-call | tf_op jit(solution)/shard_map/pallas_call | solution.py:492
  134.2 2.0 %shard_map.103 = (bf16[128,1024]{1,0:T(8,128)(2,1)}, bf16[128,1024]{1,0:T(8,128)(2,1)}, f32[32,1024]{1,0:T(8,128)}, f32[32,1024]{1,0:T(8,128)}) custom-call(bf16[128,1024]{1,0:T(8,128)(2,1)} %get-tuple-element.8.refs_0_, bf16[128,1024]{1,0:T(8,128)(2,1)} %get-tuple-element.9.refs_1_, f32[32,1024]{1,0:T(8,128)} %get-tuple-element.10.refs_2_, ...), custom_call_target="tpu_custom_call" | custom-call | tf_op jit(solution)/shard_map/pallas_call | solution.py:545

commit v3 on v2

--- a/solution.py
+++ b/solution.py
@@ -11,8 +11,11 @@
 NX, NZ, TOK, D, E = 4, 16, 128, 1024, 1024
 NC = 4
 ROWS = TOK // NC
-LATE = ((0, 1), (2, 3))
-AHEAD = ((2, 3), (0, 1))
+HALF = TOK // 2
+LATE = ((0, 2), (1, 3))
+AHEAD = ((1, 3), (0, 2))
+COLUMNS = ((2, 1), (2, 0), (1, 1), (3, 1), (1, 0), (3, 0), (0, 1))
+ALL_GRP = tuple((1,) + p for p in COLUMNS) + ((1, 0, 0),) + tuple((0,) + p for p in COLUMNS)
 CLIP, TEXT = 0, 1
 
 
@@ -26,8 +29,7 @@
     shift_ref,
     clip_hid,
     text_hid,
-    clip_wg,
-    text_wg,
+    f_all,
     w,
     hx,
     ht,
@@ -41,15 +43,16 @@
     back_out,
     share_out,
     share_in,
+    raw_out,
     g_out,
     g_in,
+    w_first,
     y_out,
     y_in,
     z_out,
     z_in,
-    f_in,
+    f_own,
     hid_out,
-    wg_out,
     load_sem,
     out_sem,
     ring_s,
@@ -238,14 +241,15 @@
     share_grad = remote(share_out, share_in, share_s.at[1], share_r.at[1], partner)
     share_grad.start()
 
-    def ga_copy(tower, o, wait=False):
-        to = (q + o) % 8
-        return remote(
-            g_out.at[tower, to],
-            g_in.at[tower, (q - o + 8) % 8 if wait else q],
-            ga_s.at[tower, o - 1],
-            ga_r.at[tower, o - 1],
-            place(x=to // 2, core=to % 2),
+    def ga_copy(tower, h, dx, dc, wait=False):
+        to = ((x + dx) % 4) * 2 + (core + dc) % 2
+        come = ((x - dx + 4) % 4) * 2 + (core + dc) % 2
+        return remote(
+            g_out.at[tower, h, to],
+            g_in.at[tower, h, come if wait else q],
+            ga_s.at[tower, h, dx * 2 + dc - 1],
+            ga_r.at[tower, h, dx * 2 + dc - 1],
+            place(x=(x + dx) % 4, core=(core + dc) % 2),
         )
 
     def yb_copy(tower, o):
@@ -270,31 +274,26 @@
             z_out.at[tower, rest], z_in.at[tower, rest], zc_s.at[tower], zc_r.at[tower], right
         )
 
-    def fd_copy(tower, o):
-        return remote(
-            f_in.at[tower, 0],
-            f_in.at[tower, o],
-            fd_s.at[tower],
-            fd_r.at[tower],
-            ((grp + o) % 16, blk),
+    def fd_copy(tower, dy, dx, dc):
+        to = ((yh + dy) % 2) * 8 + ((x + dx) % 4) * 2 + (core + dc) % 2
+        return remote(
+            f_own.at[tower], f_all.at[tower, grp], fd_s.at[tower], fd_r.at[tower], (to, blk)
         )
 
     def fd_all(tower):
-        rest = pl.ds(1, 15)
-        return remote(
-            f_in.at[tower, rest], f_in.at[tower, rest], fd_s.at[tower], fd_r.at[tower], right
-        )
-
-    def raw_grad(tower, grad):
-        vec = unit[tower]
+        rest = f_all.at[tower, pl.ds(0, 15)]
+        return remote(rest, rest, fd_s.at[tower], fd_r.at[tower], right)
+
+    def raw_grad(tower, h, grad):
+        rows = pl.ds(HALF * h, HALF)
+        vec = unit[tower, rows]
         radial = jnp.sum(vec * grad, axis=1, keepdims=True)
-        raw = ((grad - vec * radial) / length[tower]).astype(BF16)
+        raw = ((grad - vec * radial) / length[tower, rows]).astype(BF16)
         for j in range(8):
-            g_out[tower, j] = raw[:, 128 * j : 128 * (j + 1)]
-
-        @pl.loop(1, 8)
-        def _(o):
-            ga_copy(tower, o).start()
+            g_out[tower, h, j] = raw[:, 128 * j : 128 * (j + 1)]
+        for dx, dc in COLUMNS:
+            ga_copy(tower, h, dx, dc).start()
+        raw_out[tower, rows] = raw
 
     def hidden_copy(tower):
         return pltpu.make_async_copy(
@@ -302,28 +301,34 @@
         )
 
     def hidden_grad(tower):
-        raw = jnp.concatenate([g_out[tower, j] for j in range(8)], axis=1)
         hid_out[tower] = lax.dot_general(
-            raw, w[tower], (((1,), (1,)), ((), ())), preferred_element_type=F32
+            raw_out[tower], w[tower], (((1,), (1,)), ((), ())), preferred_element_type=F32
         ).astype(BF16)
         hidden_copy(tower).start()
 
-    def turn(tower, *blocks):
-        for j in blocks:
-            ht[tower, :, pl.ds(128 * j, 128)] = hx[tower, j].T
-
-    def gathered(tower):
-        g_in[tower, q] = g_out[tower, q]
-
-        @pl.loop(1, 8)
-        def _(o):
-            ga_copy(tower, o, True).wait_recv()
+    def turn(tower, h, *pairs):
+        rows = pl.ds(HALF * h, HALF)
+        for j in pairs:
+            two = jnp.concatenate([hx[tower, 2 * j, rows], hx[tower, 2 * j + 1, rows]], axis=0)
+            ht[tower, :, pl.ds(512 * h + 128 * j, 128)] = two.T
+
+    def gathered(tower, h):
+        g_in[tower, h, q] = g_out[tower, h, q]
+        for dx, dc in COLUMNS[::-1]:
+            ga_copy(tower, h, dx, dc, True).wait_recv()
+
+    def product(tower, h, rows):
+        g = g_in[tower, h].reshape(8 * HALF, 128)
+        return jnp.dot(ht[tower, rows, pl.ds(512 * h, 512)], g, preferred_element_type=F32)
+
+    def weight_first(tower):
+        gathered(tower, 0)
+        w_first[...] = product(tower, 0, pl.ds(0, D))
 
     def weight(tower, own):
         to = yl if own else 1 - yl
-        g = g_in[tower].reshape(8 * TOK, 128)
         rows = pl.ds(pl.multiple_of(512 * to, 512), 512)
-        term = jnp.dot(ht[tower, rows, :], g, preferred_element_type=F32)
+        term = w_first[rows] + product(tower, 1, rows)
         term = term.reshape(NZ, 2, 16, 128).astype(BF16)
         for yh_to in (0, 1):
             y_out[tower, yh_to * 2 + to] = term[:, yh_to]
@@ -341,24 +346,16 @@
         for o in (8, 7, 9, 6, 10, 5, 11, 4, 12, 3, 13, 2, 14, 1, 15):
             zc_copy(tower, o).start()
 
+    def own_copy(tower):
+        return pltpu.make_async_copy(f_own.at[tower], f_all.at[tower, grp], out_sem.at[2 + tower])
+
     def over_z(tower):
         z_in[tower, 0] = z_out[tower, z]
         zc_all(tower).wait_recv()
-        f_in[tower, 0] = jnp.sum(z_in[tower].astype(F32), axis=0).astype(BF16)
-        for o in range(1, 16):
-            fd_copy(tower, o).start()
-
-    def weight_copy(tower):
-        return pltpu.make_async_copy(
-            wg_out.at[tower], (clip_wg, text_wg)[tower], out_sem.at[2 + tower]
-        )
-
-    def finish(tower):
-        fd_all(tower).wait_recv()
-        for j in range(16):
-            piece = f_in[tower, (grp - j + 16) % 16].astype(F32)
-            wg_out[tower, pl.ds(16 * (j // 8), 16), pl.ds(128 * (j % 8), 128)] = piece
-        weight_copy(tower).start()
+        f_own[tower] = jnp.sum(z_in[tower].astype(F32), axis=0).astype(BF16)
+        for dy, dx, dc in ALL_GRP:
+            fd_copy(tower, dy, dx, dc).start()
+        own_copy(tower).start()
 
     def relays(tower):
         for o in (1, 2, 3):
@@ -369,9 +366,16 @@
         for o in range(4):
             relay(tower, o, True).wait_recv()
 
-    def clip_raw():
-        share_grad.wait_recv()
-        raw_grad(CLIP, cacc[pl.ds(0, TOK)] + share_in[...].astype(F32))
+    def clip_raw(h):
+        if h == 0:
+            share_grad.wait_recv()
+        rows = pl.ds(HALF * h, HALF)
+        raw_grad(CLIP, h, cacc[rows] + share_in[rows].astype(F32))
+
+    def text_raw(h):
+        rows = pl.ds(HALF * h, HALF)
+        sums = back_in[0, 0, rows].astype(F32) + back_in[1, 0, rows].astype(F32)
+        raw_grad(TEXT, h, part[0, rows] + sums)
 
     def ring_left(k):
         for d in (0, 1):
@@ -386,9 +390,9 @@
                 hid_copy(tower, o).wait_send()
 
     def columns_left(tower):
-        @pl.loop(1, 8)
-        def _(o):
-            ga_copy(tower, o).wait_send()
+        for h in (0, 1):
+            for dx, dc in COLUMNS:
+                ga_copy(tower, h, dx, dc).wait_send()
 
     def sums_left(tower):
         for o in (1, 2, 3):
@@ -398,28 +402,28 @@
         0: lambda: relays(CLIP),
         2: lambda: ring_left(1),
         3: lambda: relays_done(CLIP),
-        4: lambda: turn(CLIP, 0, 1),
-        5: lambda: turn(CLIP, 2, 3),
-        6: lambda: clip_raw(),
-        7: lambda: hidden_grad(CLIP),
-        8: lambda: turn(CLIP, 4, 5),
-        9: lambda: turn(CLIP, 6, 7),
-        10: lambda: relays(TEXT),
-        11: lambda: gathered(CLIP),
-        12: lambda: weight(CLIP, False),
+        4: lambda: turn(CLIP, 0, 0, 1),
+        5: lambda: turn(CLIP, 0, 2, 3),
+        6: lambda: clip_raw(0),
+        7: lambda: clip_raw(1),
+        8: lambda: hidden_grad(CLIP),
+        9: lambda: turn(CLIP, 1, 0, 1),
+        10: lambda: turn(CLIP, 1, 2, 3),
+        11: lambda: weight_first(CLIP),
+        12: lambda: gathered(CLIP, 1),
         13: lambda: weight(CLIP, True),
-        14: lambda: relays_done(TEXT),
-        15: lambda: turn(TEXT, 0, 1),
-        16: lambda: turn(TEXT, 2, 3),
-        17: lambda: turn(TEXT, 4, 5),
-        18: lambda: turn(TEXT, 6, 7),
-        19: lambda: over_y(CLIP),
-        20: lambda: ring_left(2),
-        21: lambda: ring_left(3),
-        22: lambda: ring_left(4),
-        23: lambda: ring_left(5),
-        24: lambda: ring_left(6),
-        25: lambda: ring_left(7),
+        14: lambda: weight(CLIP, False),
+        15: lambda: relays(TEXT),
+        16: lambda: ring_left(2),
+        17: lambda: relays_done(TEXT),
+        18: lambda: turn(TEXT, 0, 0, 1),
+        19: lambda: turn(TEXT, 0, 2, 3),
+        20: lambda: turn(TEXT, 1, 0, 1),
+        21: lambda: turn(TEXT, 1, 2, 3),
+        22: lambda: over_y(CLIP),
+        23: lambda: (ring_left(3), ring_left(4)),
+        24: lambda: ring_left(5),
+        25: lambda: (ring_left(6), ring_left(7)),
         26: lambda: ring_left(8),
     }
     for j in range(6, -1, -1):
@@ -435,14 +439,13 @@
     for i in (0, 1):
         for d in (0, 1):
             back(d, 1, LATE[d][i]).wait_recv()
-
-    grad = part[0, pl.ds(0, TOK)] + back_in[0, 0].astype(F32) + back_in[1, 0].astype(F32)
-    raw_grad(TEXT, grad)
+        text_raw(i)
     send_z(CLIP)
     hidden_grad(TEXT)
-    gathered(TEXT)
+    weight_first(TEXT)
+    gathered(TEXT, 1)
+    weight(TEXT, True)
     weight(TEXT, False)
-    weight(TEXT, True)
     over_z(CLIP)
     over_y(TEXT)
     send_z(TEXT)
@@ -455,27 +458,30 @@
 
         for c in LATE[d]:
             back(d, 8, c).wait_send()
-    finish(CLIP)
+    fd_all(CLIP).wait()
+    own_copy(CLIP).wait()
     hidden_left()
-    over_z(TEXT)
     share_emb.wait_send()
     share_grad.wait_send()
-    for tower in (CLIP, TEXT):
-        columns_left(tower)
-        sums_left(tower)
-        zc_all(tower).wait_send()
-    fd_all(CLIP).wait_send()
+    columns_left(CLIP)
+    sums_left(CLIP)
+    zc_all(CLIP).wait_send()
+    over_z(TEXT)
+    columns_left(TEXT)
+    sums_left(TEXT)
+    zc_all(TEXT).wait_send()
     hidden_copy(CLIP).wait()
     hidden_copy(TEXT).wait()
-    weight_copy(CLIP).wait()
-    finish(TEXT)
-    fd_all(TEXT).wait_send()
-    weight_copy(TEXT).wait()
-
-
-def hand_over(*refs):
-    for i in range(4):
-        refs[4 + i][...] = refs[i][...]
+    own_copy(TEXT).wait()
+    fd_all(TEXT).wait()
+
+
+def hand_over(clip_in, text_in, pieces, clip_hid, text_hid, clip_wg, text_wg):
+    clip_hid[...] = clip_in[...]
+    text_hid[...] = text_in[...]
+    for tower, out in ((CLIP, clip_wg), (TEXT, text_wg)):
+        for j in range(16):
+            out[pl.ds(16 * (j // 8), 16), pl.ds(128 * (j % 8), 128)] = pieces[tower, j].astype(F32)
 
 
 def local(hv, hc, wv, wc, match, multiplier, offset):
@@ -483,17 +489,13 @@
     smem = pl.BlockSpec(memory_space=pltpu.SMEM)
     anywhere = pl.BlockSpec(memory_space=pl.ANY)
     dma = pltpu.SemaphoreType.DMA
-    shapes = (
-        jax.ShapeDtypeStruct((TOK, D), BF16),
-        jax.ShapeDtypeStruct((TOK, D), BF16),
-        jax.ShapeDtypeStruct((32, E), F32),
-        jax.ShapeDtypeStruct((32, E), F32),
-    )
+    hidden = jax.ShapeDtypeStruct((TOK, D), BF16)
+    gradient = jax.ShapeDtypeStruct((32, E), F32)
     results = pl.pallas_call(
         kernel,
-        out_shape=shapes,
+        out_shape=(hidden, hidden, jax.ShapeDtypeStruct((2, 16, 16, 128), BF16)),
         in_specs=[anywhere] * 4 + [vmem, smem, smem],
-        out_specs=(anywhere,) * 4,
+        out_specs=(anywhere,) * 3,
         scratch_shapes=[
             pltpu.VMEM((2, D, E), BF16),
             pltpu.VMEM((2, 8, TOK, D), BF16),
@@ -508,15 +510,16 @@
             pltpu.VMEM((2, 8, TOK, E), BF16),
             pltpu.VMEM((TOK, E), BF16),
             pltpu.VMEM((TOK, E), BF16),
-            pltpu.VMEM((2, 8, TOK, 128), BF16),
-            pltpu.VMEM((2, 8, TOK, 128), BF16),
+            pltpu.VMEM((2, TOK, E), BF16),
+            pltpu.VMEM((2, 2, 8, HALF, 128), BF16),
+            pltpu.VMEM((2, 2, 8, HALF, 128), BF16),
+            pltpu.VMEM((D, 128), F32),
             pltpu.VMEM((2, 4, NZ, 16, 128), BF16),
             pltpu.VMEM((2, 4, NZ, 16, 128), BF16),
             pltpu.VMEM((2, NZ, 16, 128), BF16),
             pltpu.VMEM((2, NZ, 16, 128), BF16),
-            pltpu.VMEM((2, 16, 16, 128), BF16),
+            pltpu.VMEM((2, 16, 128), BF16),
             pltpu.VMEM((2, TOK, D), BF16),
-            pltpu.VMEM((2, 32, E), F32),
             dma((4,)),
             dma((4,)),
             dma((2, 8, NC)),
@@ -529,8 +532,8 @@
             dma((2, 3)),
             dma((2, 4)),
             dma((2, 4)),
-            dma((2, 7)),
-            dma((2, 7)),
+            dma((2, 2, 7)),
+            dma((2, 2, 7)),
             dma((2, 3)),
             dma((2, 3)),
             dma((2,)),
@@ -544,8 +547,8 @@
     )(hv, hc, wv, wc, match.reshape(32, TOK), multiplier, offset)
     return pl.pallas_call(
         hand_over,
-        out_shape=shapes,
-        in_specs=[vmem] * 4,
+        out_shape=(hidden, hidden, gradient, gradient),
+        in_specs=[vmem] * 3,
         out_specs=(vmem,) * 4,
     )(*results)
 

time: 136 us -> 134 us (0.985)
  Pallas kernels: 134 us -> 132 us
    pallas_call x2, Pallas kernels: 134 us -> 132 us  [the longest x1 130 us: local(): pl.pallas_call(kernel, out_shape=(hidden, hidden, jax.ShapeDtypeStruct((2...]
where the time goes in v3:
time: 134 us
  Pallas kernels  132 us (99%)
  between operations  1.93 us (1%)
    pallas_call x1, Pallas kernels, local(): pl.pallas_call(kernel, out_shape=(hidden, hidden, jax.ShapeDtypeStruct((2...  130 us

profile of v3, /device:TPU:1, one launch (start us, length us, event | category | flops | bytes accessed | tf_op | source)
XLA Modules:
  0.0 134.2 jit_solution(171450375862325483)
XLA Ops:
  1.9 130.3 %shard_map.102 = (bf16[128,1024]{1,0:T(8,128)(2,1)}, bf16[128,1024]{1,0:T(8,128)(2,1)}, bf16[2,16,16,128]{3,2,1,0:T(8,128)(2,1)}) custom-call(bf16[128,1024]{1,0:T(8,128)(2,1)} %hv_hbm.1, bf16[128,1024]{1,0:T(8,128)(2,1)} %hc_hbm.1, bf16[1024,1024]{1,0:T(8,128)(2,1)} %wv_hbm.1, bf16[1024,1024]{1,0:T(8,128)(2,1)} %wc_hbm.1, s32[32,128]{1,0:T(8,128)} %bitcast.1, ...), custom_call_target="tpu_custom_call" | custom-call | tf_op jit(solution)/shard_map/pallas_call | solution.py:494
  132.3 2.0 %shard_map.103 = (bf16[128,1024]{1,0:T(8,128)(2,1)}, bf16[128,1024]{1,0:T(8,128)(2,1)}, f32[32,1024]{1,0:T(8,128)}, f32[32,1024]{1,0:T(8,128)}) custom-call(bf16[128,1024]{1,0:T(8,128)(2,1)} %get-tuple-element.7.clip_in, bf16[128,1024]{1,0:T(8,128)(2,1)} %get-tuple-element.8.text_in, bf16[2,16,16,128]{3,2,1,0:T(8,128)(2,1)} %get-tuple-element.9.pieces), custom_call_target="tpu_custom_call" | custom-call | tf_op jit(solution)/shard_map/pallas_call | solution.py:548

commit v4 on v3

--- a/solution.py
+++ b/solution.py
@@ -24,9 +24,9 @@
     hc_hbm,
     wv_hbm,
     wc_hbm,
-    match_ref,
-    scale_ref,
-    shift_ref,
+    match_hbm,
+    scale_hbm,
+    shift_hbm,
     clip_hid,
     text_hid,
     f_all,
@@ -34,7 +34,7 @@
     hx,
     ht,
     unit,
-    length,
+    inverse,
     tt,
     emb,
     part,
@@ -51,10 +51,10 @@
     y_in,
     z_out,
     z_in,
-    f_own,
-    hid_out,
+    match_ref,
+    scale_ref,
+    shift_ref,
     load_sem,
-    out_sem,
     ring_s,
     ring_r,
     back_s,
@@ -94,32 +94,37 @@
         )
 
     loads = [
-        pltpu.make_async_copy(wc_hbm, w.at[TEXT], load_sem.at[0]),
-        pltpu.make_async_copy(hc_hbm, hx.at[TEXT, q], load_sem.at[1]),
+        pltpu.make_async_copy(hc_hbm, hx.at[TEXT, q], load_sem.at[0]),
+        pltpu.make_async_copy(wc_hbm, w.at[TEXT], load_sem.at[1]),
         pltpu.make_async_copy(wv_hbm, w.at[CLIP], load_sem.at[2]),
         pltpu.make_async_copy(hv_hbm, hx.at[CLIP, q], load_sem.at[3]),
+        pltpu.make_async_copy(match_hbm, match_ref, load_sem.at[4]),
+        pltpu.make_async_copy(scale_hbm, scale_ref, load_sem.at[5]),
+        pltpu.make_async_copy(shift_hbm, shift_ref, load_sem.at[6]),
     ]
-    for copy in loads:
-        copy.start()
 
     barrier = pltpu.get_barrier_semaphore()
     near = [right, left, sibling]
     near += [place(x=(x + o) % 4) for o in (1, 2, 3)] + [place(y=(y + o) % 4) for o in (1, 2, 3)]
     for device in near:
         pl.semaphore_signal(barrier, 1, device_id=device, device_id_type=MESH)
+    loads[0].start()
+    loads[1].start()
 
     def project(tower):
         raw = jnp.dot(hx[tower, q], w[tower], preferred_element_type=F32)
         size = jnp.sqrt(jnp.sum(raw * raw, axis=1, keepdims=True) + 1e-06)
-        vec = raw / size
+        vec = raw * (1.0 / size)
         unit[tower] = vec
-        length[tower] = size
+        inverse[tower] = 1.0 / size
         return vec.astype(BF16)
 
     def ring(d, k, c):
         first = isinstance(k, int) and k == 1
         last = isinstance(k, int) and k == 8
         src = tt.at[k - 1, pl.ds((0 if first else TOK * d) + ROWS * c, ROWS)]
+        if first and c in AHEAD[d]:
+            src = hx.at[TEXT, q, pl.ds(ROWS * c, ROWS)]
         dst = tt.at[k, pl.ds((0 if last else TOK * d) + ROWS * c, ROWS)]
         return remote(src, dst, ring_s.at[d, k - 1, c], ring_r.at[d, k - 1, c], (right, left)[d])
 
@@ -150,12 +155,27 @@
         )
 
     loads[0].wait()
+    pl.semaphore_wait(barrier, len(near))
+    for i in (0, 1):
+        for d in (0, 1):
+            ring(d, 1, AHEAD[d][i]).start()
     loads[1].wait()
+    for copy in loads[2:]:
+        copy.start()
     tt[0, pl.ds(0, TOK)] = project(TEXT)
-    pl.semaphore_wait(barrier, len(near))
-    for i in range(NC):
-        for d in (0, 1):
-            ring(d, 1, (LATE[d] + AHEAD[d])[i]).start()
+    for i in (0, 1):
+        for d in (0, 1):
+            ring(d, 1, LATE[d][i]).start()
+
+    def forward(k, chunks):
+        for i in (0, 1):
+            for d in (0, 1):
+                c = chunks[d][i]
+                ring(d, k, c).wait_recv()
+                if not (isinstance(k, int) and k == 7 and c in AHEAD[d]):
+                    ring(d, k + 1, c).start()
+
+    forward(1, AHEAD)
     loads[2].wait()
     loads[3].wait()
     emb[pl.ds(0, TOK)] = project(CLIP)
@@ -168,13 +188,29 @@
             hid_copy(tower, o).start()
         relay(tower, 0).start()
 
+    for copy in loads[4:]:
+        copy.wait()
     scale = scale_ref[0]
     shift = shift_ref[0]
+
+    def embeddings(k):
+        chunks = [tt[k, pl.ds(ROWS * c, ROWS)] for c in range(2 * NC)]
+        hidden = [c for c in range(2 * NC) if c % NC in AHEAD[c // NC]]
+        raw = jnp.dot(
+            jnp.concatenate([chunks[c] for c in hidden], axis=0),
+            w[TEXT],
+            preferred_element_type=F32,
+        )
+        size = jnp.sqrt(jnp.sum(raw * raw, axis=1, keepdims=True) + 1e-06)
+        vec = (raw * (1.0 / size)).astype(BF16)
+        for i, c in enumerate(hidden):
+            chunks[c] = vec[ROWS * i : ROWS * (i + 1)]
+        return jnp.concatenate(chunks, axis=0)
 
     def work(k, rows):
         base0 = (yl * NZ + (z - k + NZ) % NZ) * TOK
         base1 = (yl * NZ + (z + k) % NZ) * TOK
-        t = tt[k, pl.ds(0, rows)]
+        t = embeddings(k) if rows == 2 * TOK else tt[k, pl.ds(0, rows)]
         a = emb[...]
         scores = scale * lax.dot_general(
             t, a, (((1,), (1,)), ((), ())), preferred_element_type=F32
@@ -190,22 +226,15 @@
         part[k, pl.ds(0, rows)] = jnp.dot(coef, a, preferred_element_type=F32)
         return lax.dot_general(coef, t, (((0,), (0,)), ((), ())), preferred_element_type=F32)
 
-    def forward(k):
-        for i in range(NC):
-            for d in (0, 1):
-                c = (LATE[d] + AHEAD[d])[i]
-                ring(d, k, c).wait_recv()
-                if not (isinstance(k, int) and k == 7 and c in AHEAD[d]):
-                    ring(d, k + 1, c).start()
-
-    forward(1)
+    forward(1, LATE)
     share_emb.wait_recv()
     cacc[...] = work(0, TOK)
 
     @pl.loop(2, 7)
     def _(k):
-        forward(k)
+        forward(k, AHEAD)
         cacc[...] += work(k - 1, 2 * TOK)
+        forward(k, LATE)
 
     def run(d, k, c):
         return part[k, pl.ds((0 if k == 8 else TOK * d) + ROWS * c, ROWS)]
@@ -220,11 +249,10 @@
         back_out[d, k - 1, rows] = (run(d, k, c) + back_in[d, k, rows].astype(F32)).astype(BF16)
         back(d, k, c).start()
 
-    forward(7)
-
-    @pl.loop(6, 8)
-    def _(k):
-        cacc[...] += work(k, 2 * TOK)
+    forward(7, AHEAD)
+    cacc[...] += work(6, 2 * TOK)
+    forward(7, LATE)
+    cacc[...] += work(7, 2 * TOK)
 
     for i in (0, 1):
         for d in (0, 1):
@@ -277,7 +305,7 @@
     def fd_copy(tower, dy, dx, dc):
         to = ((yh + dy) % 2) * 8 + ((x + dx) % 4) * 2 + (core + dc) % 2
         return remote(
-            f_own.at[tower], f_all.at[tower, grp], fd_s.at[tower], fd_r.at[tower], (to, blk)
+            f_all.at[tower, grp], f_all.at[tower, grp], fd_s.at[tower], fd_r.at[tower], (to, blk)
         )
 
     def fd_all(tower):
@@ -288,23 +316,17 @@
         rows = pl.ds(HALF * h, HALF)
         vec = unit[tower, rows]
         radial = jnp.sum(vec * grad, axis=1, keepdims=True)
-        raw = ((grad - vec * radial) / length[tower, rows]).astype(BF16)
+        raw = ((grad - vec * radial) * inverse[tower, rows]).astype(BF16)
         for j in range(8):
             g_out[tower, h, j] = raw[:, 128 * j : 128 * (j + 1)]
         for dx, dc in COLUMNS:
             ga_copy(tower, h, dx, dc).start()
         raw_out[tower, rows] = raw
 
-    def hidden_copy(tower):
-        return pltpu.make_async_copy(
-            hid_out.at[tower], (clip_hid, text_hid)[tower], out_sem.at[tower]
-        )
-
     def hidden_grad(tower):
-        hid_out[tower] = lax.dot_general(
+        (clip_hid, text_hid)[tower][...] = lax.dot_general(
             raw_out[tower], w[tower], (((1,), (1,)), ((), ())), preferred_element_type=F32
         ).astype(BF16)
-        hidden_copy(tower).start()
 
     def turn(tower, h, *pairs):
         rows = pl.ds(HALF * h, HALF)
@@ -346,16 +368,12 @@
         for o in (8, 7, 9, 6, 10, 5, 11, 4, 12, 3, 13, 2, 14, 1, 15):
             zc_copy(tower, o).start()
 
-    def own_copy(tower):
-        return pltpu.make_async_copy(f_own.at[tower], f_all.at[tower, grp], out_sem.at[2 + tower])
-
     def over_z(tower):
         z_in[tower, 0] = z_out[tower, z]
         zc_all(tower).wait_recv()
-        f_own[tower] = jnp.sum(z_in[tower].astype(F32), axis=0).astype(BF16)
+        f_all[tower, grp] = jnp.sum(z_in[tower].astype(F32), axis=0).astype(BF16)
         for dy, dx, dc in ALL_GRP:
             fd_copy(tower, dy, dx, dc).start()
-        own_copy(tower).start()
 
     def relays(tower):
         for o in (1, 2, 3):
@@ -446,9 +464,9 @@
     gathered(TEXT, 1)
     weight(TEXT, True)
     weight(TEXT, False)
-    over_z(CLIP)
     over_y(TEXT)
     send_z(TEXT)
+    over_z(CLIP)
     for d in (0, 1):
         for c in range(NC):
 
@@ -459,7 +477,6 @@
         for c in LATE[d]:
             back(d, 8, c).wait_send()
     fd_all(CLIP).wait()
-    own_copy(CLIP).wait()
     hidden_left()
     share_emb.wait_send()
     share_grad.wait_send()
@@ -470,32 +487,42 @@
     columns_left(TEXT)
     sums_left(TEXT)
     zc_all(TEXT).wait_send()
-    hidden_copy(CLIP).wait()
-    hidden_copy(TEXT).wait()
-    own_copy(TEXT).wait()
     fd_all(TEXT).wait()
 
 
-def hand_over(clip_in, text_in, pieces, clip_hid, text_hid, clip_wg, text_wg):
-    clip_hid[...] = clip_in[...]
-    text_hid[...] = text_in[...]
-    for tower, out in ((CLIP, clip_wg), (TEXT, text_wg)):
+def hand_over(clip_in, text_in, pieces, clip_hid, text_hid, clip_wg, text_wg, placed, sem):
+    copies = [
+        pltpu.make_async_copy(clip_in, clip_hid, sem.at[0]),
+        pltpu.make_async_copy(text_in, text_hid, sem.at[1]),
+        pltpu.make_async_copy(placed.at[CLIP], clip_wg, sem.at[2]),
+        pltpu.make_async_copy(placed.at[TEXT], text_wg, sem.at[3]),
+    ]
+    copies[0].start()
+    copies[1].start()
+    for tower in (CLIP, TEXT):
         for j in range(16):
-            out[pl.ds(16 * (j // 8), 16), pl.ds(128 * (j % 8), 128)] = pieces[tower, j].astype(F32)
+            rows, columns = pl.ds(16 * (j // 8), 16), pl.ds(128 * (j % 8), 128)
+            placed[tower, rows, columns] = pieces[tower, j].astype(F32)
+        copies[2 + tower].start()
+    for copy in copies:
+        copy.wait()
 
 
 def local(hv, hc, wv, wc, match, multiplier, offset):
     vmem = pl.BlockSpec(memory_space=pltpu.VMEM)
-    smem = pl.BlockSpec(memory_space=pltpu.SMEM)
     anywhere = pl.BlockSpec(memory_space=pl.ANY)
     dma = pltpu.SemaphoreType.DMA
     hidden = jax.ShapeDtypeStruct((TOK, D), BF16)
     gradient = jax.ShapeDtypeStruct((32, E), F32)
     results = pl.pallas_call(
         kernel,
-        out_shape=(hidden, hidden, jax.ShapeDtypeStruct((2, 16, 16, 128), BF16)),
-        in_specs=[anywhere] * 4 + [vmem, smem, smem],
-        out_specs=(anywhere,) * 3,
+        out_shape=(
+            pltpu.VMEM((TOK, D), BF16),
+            pltpu.VMEM((TOK, D), BF16),
+            pltpu.VMEM((2, 16, 16, 128), BF16),
+        ),
+        in_specs=[pl.BlockSpec(memory_space=pltpu.HBM)] * 7,
+        out_specs=(vmem,) * 3,
         scratch_shapes=[
             pltpu.VMEM((2, D, E), BF16),
             pltpu.VMEM((2, 8, TOK, D), BF16),
@@ -518,10 +545,10 @@
             pltpu.VMEM((2, 4, NZ, 16, 128), BF16),
             pltpu.VMEM((2, NZ, 16, 128), BF16),
             pltpu.VMEM((2, NZ, 16, 128), BF16),
-            pltpu.VMEM((2, 16, 128), BF16),
-            pltpu.VMEM((2, TOK, D), BF16),
-            dma((4,)),
-            dma((4,)),
+            pltpu.VMEM((32, TOK), jnp.int32),
+            pltpu.SMEM((1,), F32),
+            pltpu.SMEM((1,), F32),
+            dma((7,)),
             dma((2, 8, NC)),
             dma((2, 8, NC)),
             dma((2, 8, NC)),
@@ -542,15 +569,16 @@
             dma((2,)),
         ],
         compiler_params=pltpu.CompilerParams(
-            collective_id=0, has_side_effects=True, vmem_limit_bytes=60 << 20
+            collective_id=0, has_side_effects=True, vmem_limit_bytes=56 << 20
         ),
     )(hv, hc, wv, wc, match.reshape(32, TOK), multiplier, offset)
     return pl.pallas_call(
         hand_over,
         out_shape=(hidden, hidden, gradient, gradient),
         in_specs=[vmem] * 3,
-        out_specs=(vmem,) * 4,
-    )(*results)
+        out_specs=(anywhere,) * 4,
+        scratch_shapes=[pltpu.VMEM((2, 32, E), F32), dma((4,))],
+    )(*(pltpu.with_memory_space_constraint(a, pltpu.VMEM) for a in results))
 
 
 def solution(mesh):

time: 134 us -> 132 us (0.985)
  Pallas kernels: 132 us -> 130 us
    pallas_call x1, Pallas kernels: 130 us -> 129 us  [local(): pl.pallas_call(kernel, out_shape=(pltpu.VMEM((TOK, D), BF16), pltpu.VMEM(...]
where the time goes in v4:
time: 132 us
  Pallas kernels  130 us (98%)
  between operations  1.93 us (1%)
    pallas_call x1, Pallas kernels, local(): pl.pallas_call(kernel, out_shape=(pltpu.VMEM((TOK, D), BF16), pltpu.VMEM(...  129 us

profile of v4, /device:TPU:1, one launch (start us, length us, event | category | flops | bytes accessed | tf_op | source)
XLA Modules:
  0.0 131.8 jit_solution(5641376049208541203)
XLA Ops:
  1.9 129.0 %shard_map.102 = (bf16[128,1024]{1,0:T(8,128)(2,1)S(1)}, bf16[128,1024]{1,0:T(8,128)(2,1)S(1)}, bf16[2,16,16,128]{3,2,1,0:T(8,128)(2,1)S(1)}) custom-call(bf16[128,1024]{1,0:T(8,128)(2,1)} %hv_hbm.1, bf16[128,1024]{1,0:T(8,128)(2,1)} %hc_hbm.1, bf16[1024,1024]{1,0:T(8,128)(2,1)} %wv_hbm.1, bf16[1024,1024]{1,0:T(8,128)(2,1)} %wc_hbm.1, s32[32,128]{1,0:T(8,128)} %bitcast.1, ...), custom_call_target="tpu_custom_call" | custom-call | tf_op jit(solution)/shard_map/pallas_call | solution.py:517
  130.9 0.9 shard_map.103

commit v5 on v4

--- a/solution.py
+++ b/solution.py
@@ -126,33 +126,44 @@
         if first and c in AHEAD[d]:
             src = hx.at[TEXT, q, pl.ds(ROWS * c, ROWS)]
         dst = tt.at[k, pl.ds((0 if last else TOK * d) + ROWS * c, ROWS)]
-        return remote(src, dst, ring_s.at[d, k - 1, c], ring_r.at[d, k - 1, c], (right, left)[d])
+        return remote(src, dst, ring_s.at[d], ring_r.at[d, k - 1, c], (right, left)[d])
 
     def back(d, k, c):
         rows = pl.ds(ROWS * c, ROWS)
         return remote(
             back_out.at[d, k - 1, rows],
             back_in.at[d, k - 1, rows],
-            back_s.at[d, k - 1, c],
+            back_s.at[d],
             back_r.at[d, k - 1, c],
             (left, right)[d],
         )
 
-    def hid_copy(tower, o, wait=False):
-        index = ((x - o + 4) % 4) * 2 + core if wait else q
-        return remote(
-            hx.at[tower, index],
-            hx.at[tower, index],
-            hid_s.at[tower, o - 1],
-            hid_r.at[tower, o - 1],
+    def hid_copy(tower, o):
+        return remote(
+            hx.at[tower, q],
+            hx.at[tower, q],
+            hid_s.at[tower],
+            hid_r.at[tower],
             place(x=(x + o) % NX),
         )
 
-    def relay(tower, o, wait=False):
-        index = ((x - o + 4) % 4) * 2 + ((1 - core) if wait else core)
-        return remote(
-            hx.at[tower, index], hx.at[tower, index], rel_s.at[tower, o], rel_r.at[tower, o], sibling
-        )
+    def relay(tower, o):
+        index = ((x - o + 4) % 4) * 2 + core
+        return remote(
+            hx.at[tower, index], hx.at[tower, index], rel_s.at[tower], rel_r.at[tower], sibling
+        )
+
+    def ring_all(d, sems):
+        chunks = tt.at[pl.ds(0, 5), pl.ds(0, 192)]
+        return remote(chunks, chunks, sems.at[d], ring_r.at[d, 0, 0], right)
+
+    def hid_all(tower):
+        blocks = hx.at[tower, pl.ds(0, 3)]
+        return remote(blocks, blocks, hid_s.at[tower], hid_r.at[tower], right)
+
+    def relay_all(tower):
+        blocks = hx.at[tower, pl.ds(0, 4)]
+        return remote(blocks, blocks, rel_s.at[tower], rel_r.at[tower], sibling)
 
     loads[0].wait()
     pl.semaphore_wait(barrier, len(near))
@@ -269,25 +280,34 @@
     share_grad = remote(share_out, share_in, share_s.at[1], share_r.at[1], partner)
     share_grad.start()
 
-    def ga_copy(tower, h, dx, dc, wait=False):
+    def ga_copy(tower, h, dx, dc):
         to = ((x + dx) % 4) * 2 + (core + dc) % 2
-        come = ((x - dx + 4) % 4) * 2 + (core + dc) % 2
         return remote(
             g_out.at[tower, h, to],
-            g_in.at[tower, h, come if wait else q],
-            ga_s.at[tower, h, dx * 2 + dc - 1],
-            ga_r.at[tower, h, dx * 2 + dc - 1],
+            g_in.at[tower, h, q],
+            ga_s.at[tower],
+            ga_r.at[tower, h],
             place(x=(x + dx) % 4, core=(core + dc) % 2),
         )
 
     def yb_copy(tower, o):
         to = (y + o) % 4
         return remote(
-            y_out.at[tower, to],
-            y_in.at[tower, o],
-            yb_s.at[tower, o - 1],
-            yb_r.at[tower, o - 1],
-            place(y=to),
+            y_out.at[tower, to], y_in.at[tower, o], yb_s.at[tower], yb_r.at[tower], place(y=to)
+        )
+
+    def ga_half(tower, h):
+        parts = g_in.at[tower, h, pl.ds(0, 7)]
+        return remote(parts, parts, ga_s.at[tower], ga_r.at[tower, h], sibling)
+
+    def ga_both(tower):
+        parts = g_out.at[tower, :, pl.ds(0, 7)]
+        return remote(parts, parts, ga_s.at[tower], ga_r.at[tower, 0], sibling)
+
+    def yb_all(tower):
+        rest = pl.ds(1, 3)
+        return remote(
+            y_out.at[tower, rest], y_in.at[tower, rest], yb_s.at[tower], yb_r.at[tower], partner
         )
 
     def zc_copy(tower, o):
@@ -336,8 +356,7 @@
 
     def gathered(tower, h):
         g_in[tower, h, q] = g_out[tower, h, q]
-        for dx, dc in COLUMNS[::-1]:
-            ga_copy(tower, h, dx, dc, True).wait_recv()
+        ga_half(tower, h).wait_recv()
 
     def product(tower, h, rows):
         g = g_in[tower, h].reshape(8 * HALF, 128)
@@ -358,9 +377,9 @@
             yb_copy(tower, o).start()
 
     def over_y(tower):
+        yb_all(tower).wait_recv()
         total = y_out[tower, y].astype(F32)
-        for o in (1, 3, 2):
-            yb_copy(tower, o).wait_recv()
+        for o in (1, 2, 3):
             total = total + y_in[tower, o].astype(F32)
         z_out[tower] = total.astype(BF16)
 
@@ -376,13 +395,9 @@
             fd_copy(tower, dy, dx, dc).start()
 
     def relays(tower):
+        hid_all(tower).wait_recv()
         for o in (1, 2, 3):
-            hid_copy(tower, o, True).wait_recv()
             relay(tower, o).start()
-
-    def relays_done(tower):
-        for o in range(4):
-            relay(tower, o, True).wait_recv()
 
     def clip_raw(h):
         if h == 0:
@@ -395,31 +410,9 @@
         sums = back_in[0, 0, rows].astype(F32) + back_in[1, 0, rows].astype(F32)
         raw_grad(TEXT, h, part[0, rows] + sums)
 
-    def ring_left(k):
-        for d in (0, 1):
-            for c in range(NC) if k < 8 else LATE[d]:
-                ring(d, k, c).wait_send()
-
-    def hidden_left():
-        for tower in (CLIP, TEXT):
-            for o in range(4):
-                relay(tower, o).wait_send()
-            for o in (1, 2, 3):
-                hid_copy(tower, o).wait_send()
-
-    def columns_left(tower):
-        for h in (0, 1):
-            for dx, dc in COLUMNS:
-                ga_copy(tower, h, dx, dc).wait_send()
-
-    def sums_left(tower):
-        for o in (1, 2, 3):
-            yb_copy(tower, o).wait_send()
-
     pieces = {
         0: lambda: relays(CLIP),
-        2: lambda: ring_left(1),
-        3: lambda: relays_done(CLIP),
+        3: lambda: relay_all(CLIP).wait_recv(),
         4: lambda: turn(CLIP, 0, 0, 1),
         5: lambda: turn(CLIP, 0, 2, 3),
         6: lambda: clip_raw(0),
@@ -432,17 +425,14 @@
         13: lambda: weight(CLIP, True),
         14: lambda: weight(CLIP, False),
         15: lambda: relays(TEXT),
-        16: lambda: ring_left(2),
-        17: lambda: relays_done(TEXT),
+        17: lambda: relay_all(TEXT).wait_recv(),
         18: lambda: turn(TEXT, 0, 0, 1),
         19: lambda: turn(TEXT, 0, 2, 3),
         20: lambda: turn(TEXT, 1, 0, 1),
         21: lambda: turn(TEXT, 1, 2, 3),
         22: lambda: over_y(CLIP),
-        23: lambda: (ring_left(3), ring_left(4)),
-        24: lambda: ring_left(5),
-        25: lambda: (ring_left(6), ring_left(7)),
-        26: lambda: ring_left(8),
+        24: lambda: ring_all(0, ring_s).wait_send(),
+        25: lambda: ring_all(1, ring_s).wait_send(),
     }
     for j in range(6, -1, -1):
         for i in range(4):
@@ -468,25 +458,18 @@
     send_z(TEXT)
     over_z(CLIP)
     for d in (0, 1):
-        for c in range(NC):
-
-            @pl.loop(1, 8)
-            def _(k):
-                back(d, k, c).wait_send()
-
-        for c in LATE[d]:
-            back(d, 8, c).wait_send()
-    fd_all(CLIP).wait()
-    hidden_left()
+        ring_all(d, back_s).wait_send()
     share_emb.wait_send()
     share_grad.wait_send()
-    columns_left(CLIP)
-    sums_left(CLIP)
+    for tower in (CLIP, TEXT):
+        hid_all(tower).wait_send()
+        relay_all(tower).wait_send()
+        ga_both(tower).wait_send()
+        yb_all(tower).wait_send()
     zc_all(CLIP).wait_send()
     over_z(TEXT)
-    columns_left(TEXT)
-    sums_left(TEXT)
     zc_all(TEXT).wait_send()
+    fd_all(CLIP).wait()
     fd_all(TEXT).wait()
 
 
@@ -549,20 +532,20 @@
             pltpu.SMEM((1,), F32),
             pltpu.SMEM((1,), F32),
             dma((7,)),
+            dma((2,)),
             dma((2, 8, NC)),
+            dma((2,)),
             dma((2, 8, NC)),
-            dma((2, 8, NC)),
-            dma((2, 8, NC)),
-            dma((2,)),
-            dma((2,)),
-            dma((2, 3)),
-            dma((2, 3)),
-            dma((2, 4)),
-            dma((2, 4)),
-            dma((2, 2, 7)),
-            dma((2, 2, 7)),
-            dma((2, 3)),
-            dma((2, 3)),
+            dma((2,)),
+            dma((2,)),
+            dma((2,)),
+            dma((2,)),
+            dma((2,)),
+            dma((2,)),
+            dma((2,)),
+            dma((2, 2)),
+            dma((2,)),
+            dma((2,)),
             dma((2,)),
             dma((2,)),
             dma((2,)),

time: 132 us -> 130 us (0.985)
  Pallas kernels: 130 us -> 128 us
    pallas_call x1, Pallas kernels: 129 us -> 127 us  [local(): pl.pallas_call(kernel, out_shape=(pltpu.VMEM((TOK, D), BF16), pltpu.VMEM(...]
where the time goes in v5:
time: 130 us
  Pallas kernels  128 us (98%)
  between operations  1.93 us (1%)
    pallas_call x1, Pallas kernels, local(): pl.pallas_call(kernel, out_shape=(pltpu.VMEM((TOK, D), BF16), pltpu.VMEM(...  127 us

profile of v5, /device:TPU:1, one launch (start us, length us, event | category | flops | bytes accessed | tf_op | source)
XLA Modules:
  0.0 129.9 jit_solution(4331566795350935946)
XLA Ops:
  1.9 127.1 %shard_map.102 = (bf16[128,1024]{1,0:T(8,128)(2,1)S(1)}, bf16[128,1024]{1,0:T(8,128)(2,1)S(1)}, bf16[2,16,16,128]{3,2,1,0:T(8,128)(2,1)S(1)}) custom-call(bf16[128,1024]{1,0:T(8,128)(2,1)} %hv_hbm.1, bf16[128,1024]{1,0:T(8,128)(2,1)} %hc_hbm.1, bf16[1024,1024]{1,0:T(8,128)(2,1)} %wv_hbm.1, bf16[1024,1024]{1,0:T(8,128)(2,1)} %wc_hbm.1, s32[32,128]{1,0:T(8,128)} %bitcast.1, ...), custom_call_target="tpu_custom_call" | custom-call | tf_op jit(solution)/shard_map/pallas_call | solution.py:500
  129.0 0.9 shard_map.103

commit v6 on v5

--- a/solution.py
+++ b/solution.py
@@ -17,6 +17,9 @@
 COLUMNS = ((2, 1), (2, 0), (1, 1), (3, 1), (1, 0), (3, 0), (0, 1))
 ALL_GRP = tuple((1,) + p for p in COLUMNS) + ((1, 0, 0),) + tuple((0,) + p for p in COLUMNS)
 CLIP, TEXT = 0, 1
+NEAR, FAR = 0, 1
+FAR_OFFSETS = (8, 7, 9, 6, 10, 5, 11, 4)
+NEAR_OFFSETS = (12, 3, 13, 2, 14, 1, 15)
 
 
 def kernel(
@@ -290,10 +293,14 @@
             place(x=(x + dx) % 4, core=(core + dc) % 2),
         )
 
-    def yb_copy(tower, o):
+    def yb_copy(tower, side, o):
         to = (y + o) % 4
         return remote(
-            y_out.at[tower, to], y_in.at[tower, o], yb_s.at[tower], yb_r.at[tower], place(y=to)
+            y_out.at[tower, side, to],
+            y_in.at[tower, side, o],
+            yb_s.at[tower],
+            yb_r.at[tower, side],
+            place(y=to),
         )
 
     def ga_half(tower, h):
@@ -304,16 +311,18 @@
         parts = g_out.at[tower, :, pl.ds(0, 7)]
         return remote(parts, parts, ga_s.at[tower], ga_r.at[tower, 0], sibling)
 
-    def yb_all(tower):
-        rest = pl.ds(1, 3)
-        return remote(
-            y_out.at[tower, rest], y_in.at[tower, rest], yb_s.at[tower], yb_r.at[tower], partner
-        )
+    def yb_side(tower, side):
+        parts = y_in.at[tower, side, pl.ds(1, 3)]
+        return remote(parts, parts, yb_s.at[tower], yb_r.at[tower, side], partner)
+
+    def yb_both(tower):
+        parts = y_out.at[tower, :, pl.ds(0, 3)]
+        return remote(parts, parts, yb_s.at[tower], yb_r.at[tower, 0], partner)
 
     def zc_copy(tower, o):
         to = (z + o) % NZ
         return remote(
-            z_out.at[tower, to], z_in.at[tower, o], zc_s.at[tower], zc_r.at[tower], place(z=to)
+            z_out.at[tower, (o + 4) % NZ], z_in.at[tower, o], zc_s.at[tower], zc_r.at[tower], place(z=to)
         )
 
     def zc_all(tower):
@@ -352,43 +361,49 @@
         rows = pl.ds(HALF * h, HALF)
         for j in pairs:
             two = jnp.concatenate([hx[tower, 2 * j, rows], hx[tower, 2 * j + 1, rows]], axis=0)
-            ht[tower, :, pl.ds(512 * h + 128 * j, 128)] = two.T
+            turned = two.T.reshape(2, NZ, 2, 16, 128)
+            columns = pl.ds(512 * h + 128 * j, 128)
+            for z_to in range(NZ):
+                s = (z_to - z + 4 + NZ) % NZ
+                for yl_to in (0, 1):
+                    for yh_to in (0, 1):
+                        ht[tower, s // 8, yh_to * 2 + yl_to, s % 8, :, columns] = turned[
+                            yl_to, z_to, yh_to
+                        ]
 
     def gathered(tower, h):
         g_in[tower, h, q] = g_out[tower, h, q]
         ga_half(tower, h).wait_recv()
 
-    def product(tower, h, rows):
+    def product(tower, h, side):
         g = g_in[tower, h].reshape(8 * HALF, 128)
-        return jnp.dot(ht[tower, rows, pl.ds(512 * h, 512)], g, preferred_element_type=F32)
+        rows = ht[tower, side, :, :, :, pl.ds(512 * h, 512)].reshape(512, 512)
+        return jnp.dot(rows, g, preferred_element_type=F32)
 
     def weight_first(tower):
         gathered(tower, 0)
-        w_first[...] = product(tower, 0, pl.ds(0, D))
-
-    def weight(tower, own):
-        to = yl if own else 1 - yl
-        rows = pl.ds(pl.multiple_of(512 * to, 512), 512)
-        term = w_first[rows] + product(tower, 1, rows)
-        term = term.reshape(NZ, 2, 16, 128).astype(BF16)
-        for yh_to in (0, 1):
-            y_out[tower, yh_to * 2 + to] = term[:, yh_to]
-        for o in (2,) if own else (1, 3):
-            yb_copy(tower, o).start()
-
-    def over_y(tower):
-        yb_all(tower).wait_recv()
-        total = y_out[tower, y].astype(F32)
+        for side in (FAR, NEAR):
+            w_first[side] = product(tower, 0, side)
+
+    def weight(tower, side):
+        term = (w_first[side] + product(tower, 1, side)).astype(BF16)
+        y_out[tower, side] = term.reshape(4, 8, 16, 128)
+        for o in (2, 1, 3):
+            yb_copy(tower, side, o).start()
+
+    def over_y(tower, side):
+        yb_side(tower, side).wait_recv()
+        total = y_out[tower, side, y].astype(F32)
         for o in (1, 2, 3):
-            total = total + y_in[tower, o].astype(F32)
-        z_out[tower] = total.astype(BF16)
-
-    def send_z(tower):
-        for o in (8, 7, 9, 6, 10, 5, 11, 4, 12, 3, 13, 2, 14, 1, 15):
+            total = total + y_in[tower, side, o].astype(F32)
+        z_out[tower, pl.ds(8 * side, 8)] = total.astype(BF16)
+
+    def send_z(tower, side):
+        for o in (FAR_OFFSETS if side == FAR else NEAR_OFFSETS):
             zc_copy(tower, o).start()
 
     def over_z(tower):
-        z_in[tower, 0] = z_out[tower, z]
+        z_in[tower, 0] = z_out[tower, 4]
         zc_all(tower).wait_recv()
         f_all[tower, grp] = jnp.sum(z_in[tower].astype(F32), axis=0).astype(BF16)
         for dy, dx, dc in ALL_GRP:
@@ -411,28 +426,32 @@
         raw_grad(TEXT, h, part[0, rows] + sums)
 
     pieces = {
-        0: lambda: relays(CLIP),
-        3: lambda: relay_all(CLIP).wait_recv(),
-        4: lambda: turn(CLIP, 0, 0, 1),
-        5: lambda: turn(CLIP, 0, 2, 3),
+        0: lambda: (relays(CLIP), relays(TEXT)),
+        2: lambda: (relay_all(CLIP).wait_recv(), turn(CLIP, 0, 0)),
+        3: lambda: turn(CLIP, 0, 1),
+        4: lambda: turn(CLIP, 0, 2),
+        5: lambda: turn(CLIP, 0, 3),
         6: lambda: clip_raw(0),
         7: lambda: clip_raw(1),
         8: lambda: hidden_grad(CLIP),
-        9: lambda: turn(CLIP, 1, 0, 1),
-        10: lambda: turn(CLIP, 1, 2, 3),
-        11: lambda: weight_first(CLIP),
-        12: lambda: gathered(CLIP, 1),
-        13: lambda: weight(CLIP, True),
-        14: lambda: weight(CLIP, False),
-        15: lambda: relays(TEXT),
-        17: lambda: relay_all(TEXT).wait_recv(),
-        18: lambda: turn(TEXT, 0, 0, 1),
-        19: lambda: turn(TEXT, 0, 2, 3),
-        20: lambda: turn(TEXT, 1, 0, 1),
-        21: lambda: turn(TEXT, 1, 2, 3),
-        22: lambda: over_y(CLIP),
-        24: lambda: ring_all(0, ring_s).wait_send(),
-        25: lambda: ring_all(1, ring_s).wait_send(),
+        9: lambda: turn(CLIP, 1, 0),
+        10: lambda: turn(CLIP, 1, 1),
+        11: lambda: turn(CLIP, 1, 2),
+        12: lambda: turn(CLIP, 1, 3),
+        13: lambda: weight_first(CLIP),
+        14: lambda: (gathered(CLIP, 1), weight(CLIP, FAR)),
+        15: lambda: weight(CLIP, NEAR),
+        16: lambda: (relay_all(TEXT).wait_recv(), turn(TEXT, 0, 0)),
+        17: lambda: turn(TEXT, 0, 1),
+        18: lambda: turn(TEXT, 0, 2),
+        19: lambda: turn(TEXT, 0, 3),
+        20: lambda: turn(TEXT, 1, 0),
+        21: lambda: turn(TEXT, 1, 1),
+        22: lambda: turn(TEXT, 1, 2),
+        23: lambda: turn(TEXT, 1, 3),
+        24: lambda: (over_y(CLIP, FAR), over_y(CLIP, NEAR)),
+        25: lambda: ring_all(0, ring_s).wait_send(),
+        26: lambda: ring_all(1, ring_s).wait_send(),
     }
     for j in range(6, -1, -1):
         for i in range(4):
@@ -448,14 +467,16 @@
         for d in (0, 1):
             back(d, 1, LATE[d][i]).wait_recv()
         text_raw(i)
-    send_z(CLIP)
+    send_z(CLIP, FAR)
+    send_z(CLIP, NEAR)
     hidden_grad(TEXT)
     weight_first(TEXT)
     gathered(TEXT, 1)
-    weight(TEXT, True)
-    weight(TEXT, False)
-    over_y(TEXT)
-    send_z(TEXT)
+    for side in (FAR, NEAR):
+        weight(TEXT, side)
+    for side in (FAR, NEAR):
+        over_y(TEXT, side)
+        send_z(TEXT, side)
     over_z(CLIP)
     for d in (0, 1):
         ring_all(d, back_s).wait_send()
@@ -465,7 +486,7 @@
         hid_all(tower).wait_send()
         relay_all(tower).wait_send()
         ga_both(tower).wait_send()
-        yb_all(tower).wait_send()
+        yb_both(tower).wait_send()
     zc_all(CLIP).wait_send()
     over_z(TEXT)
     zc_all(TEXT).wait_send()
@@ -509,7 +530,7 @@
         scratch_shapes=[
             pltpu.VMEM((2, D, E), BF16),
             pltpu.VMEM((2, 8, TOK, D), BF16),
-            pltpu.VMEM((2, D, 8 * TOK), BF16),
+            pltpu.VMEM((2, 2, 4, 8, 16, 8 * TOK), BF16),
             pltpu.VMEM((2, TOK, E), F32),
             pltpu.VMEM((2, TOK, 1), F32),
             pltpu.VMEM((9, 2 * TOK, E), BF16),
@@ -523,9 +544,9 @@
             pltpu.VMEM((2, TOK, E), BF16),
             pltpu.VMEM((2, 2, 8, HALF, 128), BF16),
             pltpu.VMEM((2, 2, 8, HALF, 128), BF16),
-            pltpu.VMEM((D, 128), F32),
-            pltpu.VMEM((2, 4, NZ, 16, 128), BF16),
-            pltpu.VMEM((2, 4, NZ, 16, 128), BF16),
+            pltpu.VMEM((2, D // 2, 128), F32),
+            pltpu.VMEM((2, 2, 4, 8, 16, 128), BF16),
+            pltpu.VMEM((2, 2, 4, 8, 16, 128), BF16),
             pltpu.VMEM((2, NZ, 16, 128), BF16),
             pltpu.VMEM((2, NZ, 16, 128), BF16),
             pltpu.VMEM((32, TOK), jnp.int32),
@@ -545,7 +566,7 @@
             dma((2,)),
             dma((2, 2)),
             dma((2,)),
-            dma((2,)),
+            dma((2, 2)),
             dma((2,)),
             dma((2,)),
             dma((2,)),

time: 130 us -> 129 us (level)
  no operation moved by 1% of the time
where the time goes in v6:
time: 129 us
  Pallas kernels  127 us (98%)
  between operations  1.93 us (1%)
    pallas_call x1, Pallas kernels, local(): pl.pallas_call(kernel, out_shape=(pltpu.VMEM((TOK, D), BF16), pltpu.VMEM(...  126 us

profile of v6, /device:TPU:1, one launch (start us, length us, event | category | flops | bytes accessed | tf_op | source)
XLA Modules:
  0.0 129.0 jit_solution(2170186213817563849)
XLA Ops:
  1.9 126.2 %shard_map.102 = (bf16[128,1024]{1,0:T(8,128)(2,1)S(1)}, bf16[128,1024]{1,0:T(8,128)(2,1)S(1)}, bf16[2,16,16,128]{3,2,1,0:T(8,128)(2,1)S(1)}) custom-call(bf16[128,1024]{1,0:T(8,128)(2,1)} %hv_hbm.1, bf16[128,1024]{1,0:T(8,128)(2,1)} %hc_hbm.1, bf16[1024,1024]{1,0:T(8,128)(2,1)} %wv_hbm.1, bf16[1024,1024]{1,0:T(8,128)(2,1)} %wc_hbm.1, s32[32,128]{1,0:T(8,128)} %bitcast.1, ...), custom_call_target="tpu_custom_call" | custom-call | tf_op jit(solution)/shard_map/pallas_call | solution.py:521
  128.1 0.9 shard_map.103

commit v7 on v6

--- a/solution.py
+++ b/solution.py
@@ -469,7 +469,6 @@
         text_raw(i)
     send_z(CLIP, FAR)
     send_z(CLIP, NEAR)
-    hidden_grad(TEXT)
     weight_first(TEXT)
     gathered(TEXT, 1)
     for side in (FAR, NEAR):
@@ -477,6 +476,7 @@
     for side in (FAR, NEAR):
         over_y(TEXT, side)
         send_z(TEXT, side)
+    hidden_grad(TEXT)
     over_z(CLIP)
     for d in (0, 1):
         ring_all(d, back_s).wait_send()

time: 129 us -> 129 us (level)
  no operation moved by 1% of the time
where the time goes in v7:
time: 129 us
  Pallas kernels  127 us (98%)
  between operations  1.93 us (1%)
    pallas_call x1, Pallas kernels, local(): pl.pallas_call(kernel, out_shape=(pltpu.VMEM((TOK, D), BF16), pltpu.VMEM(...  126 us

profile of v7, /device:TPU:1, one launch (start us, length us, event | category | flops | bytes accessed | tf_op | source)
XLA Modules:
  0.0 129.0 jit_solution(556437775008515762)
XLA Ops:
  1.9 126.2 %shard_map.102 = (bf16[128,1024]{1,0:T(8,128)(2,1)S(1)}, bf16[128,1024]{1,0:T(8,128)(2,1)S(1)}, bf16[2,16,16,128]{3,2,1,0:T(8,128)(2,1)S(1)}) custom-call(bf16[128,1024]{1,0:T(8,128)(2,1)} %hv_hbm.1, bf16[128,1024]{1,0:T(8,128)(2,1)} %hc_hbm.1, bf16[1024,1024]{1,0:T(8,128)(2,1)} %wv_hbm.1, bf16[1024,1024]{1,0:T(8,128)(2,1)} %wc_hbm.1, s32[32,128]{1,0:T(8,128)} %bitcast.1, ...), custom_call_target="tpu_custom_call" | custom-call | tf_op jit(solution)/shard_map/pallas_call | solution.py:521
  128.1 0.9 shard_map.103

commit v8 on v6

--- a/solution.py
+++ b/solution.py
@@ -137,7 +137,7 @@
             back_out.at[d, k - 1, rows],
             back_in.at[d, k - 1, rows],
             back_s.at[d],
-            back_r.at[d, k - 1, c],
+            ring_r.at[d, k - 1, c] if k <= 5 else back_r.at[d, k - 6, c],
             (left, right)[d],
         )
 
@@ -556,7 +556,7 @@
             dma((2,)),
             dma((2, 8, NC)),
             dma((2,)),
-            dma((2, 8, NC)),
+            dma((2, 3, NC)),
             dma((2,)),
             dma((2,)),
             dma((2,)),

time: 129 us -> 129 us (level)
  no operation moved by 1% of the time
where the time goes in v8:
time: 129 us
  Pallas kernels  127 us (98%)
  between operations  1.93 us (1%)
    pallas_call x1, Pallas kernels, local(): pl.pallas_call(kernel, out_shape=(pltpu.VMEM((TOK, D), BF16), pltpu.VMEM(...  126 us

profile of v8, /device:TPU:1, one launch (start us, length us, event | category | flops | bytes accessed | tf_op | source)
XLA Modules:
  0.0 128.7 jit_solution(1247673700575924025)
XLA Ops:
  1.9 125.8 %shard_map.102 = (bf16[128,1024]{1,0:T(8,128)(2,1)S(1)}, bf16[128,1024]{1,0:T(8,128)(2,1)S(1)}, bf16[2,16,16,128]{3,2,1,0:T(8,128)(2,1)S(1)}) custom-call(bf16[128,1024]{1,0:T(8,128)(2,1)} %hv_hbm.1, bf16[128,1024]{1,0:T(8,128)(2,1)} %hc_hbm.1, bf16[1024,1024]{1,0:T(8,128)(2,1)} %wv_hbm.1, bf16[1024,1024]{1,0:T(8,128)(2,1)} %wc_hbm.1, s32[32,128]{1,0:T(8,128)} %bitcast.1, ...), custom_call_target="tpu_custom_call" | custom-call | tf_op jit(solution)/shard_map/pallas_call | solution.py:521
  127.8 0.9 shard_map.103
